TPU v7x, 128 devices: a whole 4x4x4 slice. The times are simulated.
128 devices in a mesh: col: 16 (over y, z_lo, core), row: 8 (over x, z_hi).
Axes of the slice: x: 4, y: 4, z: 4 (z_hi: 2, z_lo: 2; z = z_hi * 2 + z_lo), core: 2. Of those that a mesh axis runs over, the one named last changes fastest.
Arguments:
- pressure: float32 [256, 128, 128], P('col', 'row'), may hold values from -1 to 1
- water_sat: float32 [256, 128, 128], P('col', 'row'), may hold values from 0.1 to 0.35
- gas_sat: float32 [256, 128, 128], P('col', 'row'), may hold values from 0.05 to 0.3
- depth: float32 [256, 128, 128], P('col', 'row'), may hold values from 0 to 4
- pore_volume: float32 [256, 128, 128], P('col', 'row'), may hold values from 0.5 to 5
- old_mass: float32 [3, 256, 128, 128], P(None, 'col', 'row'), may hold values from 0.2 to 4
- transmissibility: float32 [3, 256, 128, 128], P(None, 'col', 'row'), may hold values from 0.5 to 5
- fault_column: int32 [128, 3, 3, 1024], P(('col', 'row')), may hold values from 0 to 255
- fault_layer: int32 [128, 3, 3, 1024], P(('col', 'row')), may hold values from 0 to 127
- fault_transmissibility: float32 [128, 3, 3, 1024], P(('col', 'row')), may hold values from 0 to 5, as said below
- perforation_cell: int32 [128, 128], P(('col', 'row')), may hold values from 0 to 32767
- well_index: float32 [128, 128], P(('col', 'row')), may hold values from 0.5 to 5
- well_pressure: float32 [128, 128], P(('col', 'row')), may hold values from -2 to 2
Outputs:
- residual: float32 [3, 256, 128, 128], P(None, 'col', 'row')
- diagonal_block: bfloat16 [9, 256, 128, 128], P(None, 'col', 'row')
- face_blocks: bfloat16 [3, 2, 9, 256, 128, 128], P(None, None, None, 'col', 'row')
- fault_blocks: bfloat16 [9, 128, 3, 3, 1024], P(None, ('col', 'row'))
- pressure_update: float32 [256, 128, 128], P('col', 'row')
Inputs may be any that keep to these rules, and one draw needn't show every extreme that they name: fault_transmissibility[d, di + 1, dj + 1, k] equals fault_transmissibility[s, 1 - di, 1 - dj, k] for s the block at offset (di, dj); in each pair's slots the used ones come first and the rest are zero; only blocks beside each other (offsets of at most one along each areal dimension) share connections; every pair of such blocks uses 1024 // 2 or more slots, and some block uses all 1024 slots with every block beside it.
All inputs are finite; a program needn't handle non-finite values.
Results may differ from a plain program's by a relative error of at most 0.001.
Values sent between devices are 32-bit elements; how exact they have to be, the bound alone decides.
A program may use at most 192 MiB of HBM per device.

v0:
```python
import jax
import jax.numpy as jnp
from jax import lax
from jax.experimental import pallas as pl
from jax.experimental.pallas import tpu as pltpu
from jax.sharding import PartitionSpec as P

F32 = jnp.float32
BF16 = jnp.bfloat16
MESH = pl.DeviceIdType.MESH
CHUNK = 256
VMEM_BYTES = 48 * 1024 * 1024


def split(x):
    hi = x.astype(BF16)
    return hi, (x - hi.astype(F32)).astype(BF16)


def cell_terms(p, sw, sg):
    oil = 1.0 - sw - sg
    bw = 1.0 + 0.05 * p
    bo = 1.0 + 0.1 * p
    bg = 1.0 + 0.4 * p
    rs = 0.5 + 0.2 * p
    w2 = sw * (sw * (1.0 / 0.3))
    o2 = oil * (oil * (1.0 / 0.8))
    g2 = sg * (sg * (1.0 / 0.05))
    mo = bo * o2
    mo_p = 0.1 * o2
    mo_o = bo * (oil * (2.0 / 0.8))
    return dict(
        mw=bw * w2,
        mo=mo,
        mg=bg * g2,
        md=rs * mo,
        mw_p=0.05 * w2,
        mw_s=bw * (sw * (2.0 / 0.3)),
        mo_p=mo_p,
        mo_o=mo_o,
        mg_p=0.4 * g2,
        mg_s=bg * (sg * (2.0 / 0.05)),
        md_p=0.2 * mo + rs * mo_p,
        md_o=rs * mo_o,
    )


def face_terms(t, a, b, pa, pb, za, zb):
    half = 0.5 * t
    hp = half * (pa - pb)
    hz = half * (za - zb)
    ww = hp - 0.1 * hz
    wo = hp - 0.08 * hz
    wg = hp - 0.02 * hz
    sum_w = a["mw"] + b["mw"]
    sum_o = a["mo"] + b["mo"]
    sum_g = a["mg"] + b["mg"]
    sum_d = a["md"] + b["md"]
    mw = half * sum_w
    mo = half * sum_o
    mgd = half * (sum_g + sum_d)
    flux = (sum_w * ww, sum_o * wo, sum_g * wg + sum_d * wo)
    return (hp, hz, mw, mo, mgd) + flux, (ww, wo, wg)


def block_rows(c, ww, wo, wg, mw, mo, mgd):
    oil = c["mo_o"] * wo
    solved = c["md_o"] * wo
    zero = jnp.zeros_like(ww)
    return (
        c["mw_p"] * ww + mw,
        c["mw_s"] * ww,
        zero,
        c["mo_p"] * wo + mo,
        -oil,
        -oil,
        c["mg_p"] * wg + c["md_p"] * wo + mgd,
        -solved,
        c["mg_s"] * wg - solved,
    )


def neighbour(d):
    a, b = lax.axis_index("col"), lax.axis_index("row")
    ta, tb = a + d // 3 - 1, b + d % 3 - 1
    na, nb = lax.axis_size("col"), lax.axis_size("row")
    there = (ta >= 0) & (ta < na) & (tb >= 0) & (tb < nb)
    return there, (ta, tb)


def eight(body):
    def step(e, carry):
        body(jnp.where(e >= 4, e + 1, e))
        return carry

    lax.fori_loop(0, 8, step, 0)


SIDES = (7, 1, 5, 3)


def greet():
    barrier = pltpu.get_barrier_semaphore()
    count = 0
    for d in (0, 1, 2, 3, 5, 6, 7, 8):
        there, target = neighbour(d)

        @pl.when(there)
        def _():
            pl.semaphore_signal(barrier, inc=1, device_id=target, device_id_type=MESH)

        count = count + there.astype(jnp.int32)
    return barrier, count


def halo_copy(src, dst, k, count, send_sem, recv_sem):
    return pltpu.make_async_remote_copy(
        src_ref=src.at[k, pl.ds(0, count)],
        dst_ref=dst.at[k, pl.ds(0, count)],
        send_sem=send_sem.at[k],
        recv_sem=recv_sem.at[k],
        device_id=neighbour(SIDES[k])[1],
        device_id_type=MESH,
    )


def fault_copy(src, dst, d, send_sem, recv_sem, back):
    return pltpu.make_async_remote_copy(
        src_ref=src.at[d],
        dst_ref=dst.at[back],
        send_sem=send_sem.at[d],
        recv_sem=recv_sem.at[back],
        device_id=neighbour(d)[1],
        device_id_type=MESH,
    )


def wait_halos(src, dst, counts, send_sem, recv_sem):
    for k in range(4):
        copy = halo_copy(src, dst, k, counts[k], send_sem, recv_sem)
        pl.when(neighbour(SIDES[k])[0])(copy.wait_send)
        pl.when(neighbour(8 - SIDES[k])[0])(copy.wait_recv)


def wait_faults(src, dst, send_sem, recv_sem):
    def one(d):
        copy = fault_copy(src, dst, d, send_sem, recv_sem, d)

        @pl.when(neighbour(d)[0])
        def _():
            copy.wait_send()
            copy.wait_recv()

    eight(one)


def cell_rows(column, layer):
    return (column >> 4) * 8 + (column & 7), ((column >> 3) & 1) * 128 + layer


def hot(index, size):
    slots = index.shape[1]
    row = jnp.broadcast_to(index.astype(F32), (16, slots)).astype(BF16)
    iota = lax.broadcasted_iota(jnp.int32, (size, slots), 0).astype(F32).astype(BF16)
    return iota.reshape(size // 16, 16, slots) == row[None]


def hot_values(mask, value_row):
    slots = value_row.shape[1]
    hi, lo = split(jnp.broadcast_to(value_row, (16, slots)))
    zero = jnp.zeros((), BF16)
    return [jnp.where(mask, v[None], zero).reshape(128, slots) for v in (hi, lo)]


def hot_ones(mask):
    size = mask.shape[0] * 16
    return jnp.where(mask, jnp.ones((), BF16), jnp.zeros((), BF16)).reshape(size, mask.shape[2])


def as_rows(x):
    low = x[:, 0:8, :].reshape(128, 128)
    high = x[:, 8:16, :].reshape(128, 128)
    return jnp.concatenate([low, high], axis=1)


def exchange_kernel(
    p_ref, sw_ref, sg_ref, z_ref, t_ref, fc_ref, fl_ref,
    near_ref, far_ref, halo_ref,
    sbuf, rbuf, hsend, hrecv, ghi, glo, fs, fr, hs, hr,
):
    barrier, count = greet()
    fields = (p_ref, sw_ref, sg_ref, z_ref)
    for f, ref in enumerate(fields):
        hsend[0, f] = ref[15]
        hsend[1, f] = ref[0]
        hsend[2, f] = ref[:, 15, :]
        hsend[3, f] = ref[:, 0, :]
    hsend[0, 4] = t_ref[0, 15]
    hsend[2, 4] = t_ref[1, :, 15, :]
    counts = (5, 4, 5, 4)
    for k in range(4):
        there = neighbour(8 - SIDES[k])[0]

        @pl.when(jnp.logical_not(there))
        def _():
            hrecv[k] = jnp.zeros_like(hrecv[k])

    sbuf[4] = jnp.zeros_like(sbuf[4])
    rbuf[4] = jnp.zeros_like(rbuf[4])

    def clear(d):
        @pl.when(jnp.logical_not(neighbour(d)[0]))
        def _():
            rbuf[d] = jnp.zeros_like(rbuf[d])

    eight(clear)
    pl.semaphore_wait(barrier, count)
    for k in range(4):
        pl.when(neighbour(SIDES[k])[0])(halo_copy(hsend, hrecv, k, counts[k], hs, hr).start)
    for f, ref in enumerate(fields):
        hi, lo = split(as_rows(ref[...]))
        ghi[pl.ds(f * 128, 128), :] = hi
        glo[pl.ds(f * 128, 128), :] = lo

    def gather(d):
        di, dj = d // 3, d % 3
        for c in range(0, sbuf.shape[2], CHUNK):
            column = fc_ref[0, di, pl.ds(dj, 1), pl.ds(c, CHUNK)]
            layer = fl_ref[0, di, pl.ds(dj, 1), pl.ds(c, CHUNK)]
            row, lane = cell_rows(column, layer)
            pick = hot_ones(hot(lane, 256))
            lines = jnp.dot(ghi[...], pick, preferred_element_type=F32)
            lines = lines + jnp.dot(glo[...], pick, preferred_element_type=F32)
            mask = lax.broadcasted_iota(jnp.int32, (128, CHUNK), 0) == row
            for f in range(4):
                part = lines[f * 128 : (f + 1) * 128]
                sbuf[d, pl.ds(f, 1), pl.ds(c, CHUNK)] = jnp.sum(
                    jnp.where(mask, part, 0.0), axis=0, keepdims=True
                )
        pl.when(neighbour(d)[0])(fault_copy(sbuf, rbuf, d, fs, fr, 8 - d).start)

    eight(gather)
    wait_halos(hsend, hrecv, counts, hs, hr)
    for k in (0, 2):
        halo_ref[k] = hrecv[k]
        halo_ref[k + 1, 0:4] = hrecv[k + 1, 0:4]
        own = hsend[k, 4]
        halo_ref[k + 1, 4] = jnp.where(neighbour(SIDES[k])[0], own, jnp.zeros_like(own))
    wait_faults(sbuf, rbuf, fs, fr)
    for d in range(9):
        for f in range(4):
            near_ref[f, d // 3, pl.ds(d % 3, 1), :] = sbuf[d, pl.ds(f, 1), :]
            far_ref[f, d // 3, pl.ds(d % 3, 1), :] = rbuf[d, pl.ds(f, 1), :]


def terms_kernel(
    p_ref, sw_ref, sg_ref, z_ref, pv_ref, om_ref, t_ref, fc_ref, fl_ref, ft_ref,
    pc_ref, wi_ref, wp_ref, near_ref, far_ref, halo_ref,
    res_ref, diag_ref, face_ref, fault_ref, first_ref, rhs_ref, pd_ref, cond_ref, condlow_ref, fcond_ref,
    blocks, acc, wacc, lowj, chan, out_sem,
):
    slots = fc_ref.shape[3]

    def low_face(k, fields):
        a = [halo_ref[k, f] for f in range(4)]
        values, _ = face_terms(
            halo_ref[k, 4], cell_terms(*a[:3]), cell_terms(*fields[:3]), a[0], fields[0], a[3], fields[3]
        )
        condlow_ref[k // 2] = values[2] + values[3] + values[4]
        return lower_side(values)

    def lower_side(values):
        return (-values[0], -values[1], values[2], values[3], values[4]) + tuple(-v for v in values[5:])

    for v, value in enumerate(low_face(2, [r[:, 0, :] for r in (p_ref, sw_ref, sg_ref, z_ref)])):
        lowj[v] = value
    carry = low_face(0, [r[0] for r in (p_ref, sw_ref, sg_ref, z_ref)])

    row_id = lax.broadcasted_iota(jnp.int32, (16, 128), 0)
    lane_id = lax.broadcasted_iota(jnp.int32, (16, 128), 1)

    def plane(i, carry):
        refs = (p_ref, sw_ref, sg_ref, z_ref)
        own = [r[i] for r in refs]
        a = cell_terms(*own[:3])
        last = i == 15
        after = jnp.minimum(i + 1, 15)
        total = list(carry)
        out_carry = None
        for n in range(3):
            if n == 0:
                nxt = [jnp.where(last, halo_ref[1, f], r[after]) for f, r in enumerate(refs)]
                t = jnp.where(last, halo_ref[1, 4], t_ref[0, i])
            elif n == 1:
                nxt = [
                    jnp.where(row_id == 15, halo_ref[3, f, pl.ds(i, 1), :], pltpu.roll(own[f], 15, 0))
                    for f in range(4)
                ]
                t = jnp.where(row_id == 15, halo_ref[3, 4, pl.ds(i, 1), :], t_ref[1, i])
            else:
                nxt = [pltpu.roll(own[f], 127, 1) for f in range(4)]
                t = jnp.where(lane_id == 127, 0.0, t_ref[2, i])
            b = cell_terms(*nxt[:3])
            values, (ww, wo, wg) = face_terms(t, a, b, own[0], nxt[0], own[3], nxt[3])
            mw, mo, mgd = values[2:5]
            cond_ref[n, i] = mw + mo + mgd
            upper = block_rows(b, ww, wo, wg, -mw, -mo, -mgd)
            lower = block_rows(a, -ww, -wo, -wg, -mw, -mo, -mgd)
            for e in range(9):
                blocks[n, 0, e, i] = upper[e].astype(BF16)
                blocks[n, 1, e, i] = lower[e].astype(BF16)
            total = [x + y for x, y in zip(total, values)]
            below = lower_side(values)
            if n == 0:
                out_carry = below
            elif n == 1:
                for v in range(8):
                    shifted = jnp.where(row_id == 0, lowj[v, pl.ds(i, 1), :], pltpu.roll(below[v], 1, 0))
                    total[v] = total[v] + shifted
            else:
                total = [x + pltpu.roll(y, 1, 1) for x, y in zip(total, below)]
        for v in range(8):
            at = pl.multiple_of(v * 128 + i * 8, 8)
            acc[pl.ds(at, 8), 0:128] = total[v][0:8]
            acc[pl.ds(at, 8), 128:256] = total[v][8:16]
        return tuple(out_carry)

    lax.fori_loop(0, 16, plane, tuple(carry))
    out_copy = pltpu.make_async_copy(blocks, face_ref, out_sem)
    out_copy.start()

    near = [near_ref[f] for f in range(4)]
    far = [far_ref[f] for f in range(4)]
    a, b = cell_terms(*near[:3]), cell_terms(*far[:3])
    values, (ww, wo, wg) = face_terms(ft_ref[0], a, b, near[0], far[0], near[3], far[3])
    mw, mo, mgd = values[2:5]
    fcond_ref[...] = mw + mo + mgd
    for v in range(8):
        chan[v] = values[v]
    for e, value in enumerate(block_rows(b, ww, wo, wg, -mw, -mo, -mgd)):
        fault_ref[e, 0] = value.astype(BF16)

    def scatter(d):
        di, dj = d // 3, d % 3
        for c in range(0, slots, CHUNK):
            column = fc_ref[0, di, pl.ds(dj, 1), pl.ds(c, CHUNK)]
            layer = fl_ref[0, di, pl.ds(dj, 1), pl.ds(c, CHUNK)]
            row, lane = cell_rows(column, layer)
            put = hot_ones(hot(lane, 256))
            mask = hot(row, 128)
            his, los = [], []
            for v in range(8):
                hi, lo = hot_values(mask, chan[v, di, pl.ds(dj, 1), pl.ds(c, CHUNK)])
                his.append(hi)
                los.append(lo)
            weighted = jnp.concatenate(
                [jnp.concatenate(his, axis=0), jnp.concatenate(los, axis=0)], axis=1
            )
            acc[...] += lax.dot_general(
                weighted,
                jnp.concatenate([put, put], axis=1),
                (((1,), (1,)), ((), ())),
                preferred_element_type=F32,
            )

    eight(scatter)

    cell = pc_ref[...]
    row, lane = cell_rows(cell >> 7, cell & 127)
    mask = hot(row, 128)
    hi_w, lo_w = hot_values(mask, wi_ref[...])
    hi_q, lo_q = hot_values(mask, wi_ref[...] * wp_ref[...])
    weighted = jnp.concatenate(
        [jnp.concatenate([hi_w, hi_q], axis=0), jnp.concatenate([lo_w, lo_q], axis=0)], axis=1
    )
    put = hot_ones(hot(lane, 256))
    wacc[...] = lax.dot_general(
        weighted,
        jnp.concatenate([put, put], axis=1),
        (((1,), (1,)), ((), ())),
        preferred_element_type=F32,
    )

    def rows_of(ref, start):
        at = pl.multiple_of(start, 8)
        return jnp.concatenate([ref[pl.ds(at, 8), 0:128], ref[pl.ds(at, 8), 128:256]], axis=0)

    def finish(i, carry):
        p, sw, sg = p_ref[i], sw_ref[i], sg_ref[i]
        c = cell_terms(p, sw, sg)
        hp, hz, mw, mo, mgd, rw, ro, rg = [rows_of(acc, v * 128 + i * 8) for v in range(8)]
        well = rows_of(wacc, i * 8)
        drive = rows_of(wacc, 128 + i * 8) - p * well
        oil = 1.0 - sw - sg
        pv = pv_ref[i]
        rock = 2.0 * (pv * (1.0 + 0.02 * p))
        rock_p = 0.04 * pv
        bw, bo, bg, rs = 1.0 + 0.05 * p, 1.0 + 0.1 * p, 1.0 + 0.4 * p, 0.5 + 0.2 * p
        ob = oil * bo
        gas = sg * bg + rs * ob
        r0 = rock * sw * bw - 2.0 * om_ref[0, i] + rw - drive * c["mw"]
        r1 = rock * ob - 2.0 * om_ref[1, i] + ro - drive * c["mo"]
        r2 = rock * gas - 2.0 * om_ref[2, i] + rg - drive * (c["mg"] + c["md"])
        res_ref[0, i], res_ref[1, i], res_ref[2, i] = r0, r1, r2
        a0 = rock_p * sw * bw + rock * sw * 0.05
        a3 = rock_p * ob + rock * oil * 0.1
        a6 = rock_p * gas + rock * (0.4 * sg + 0.2 * ob + 0.1 * rs * oil)
        total = c["mw"] + c["mo"] + c["mg"] + c["md"]
        pd = a0 + a3 + a6 + mw + mo + mgd + well * total
        dw = hp - 0.1 * hz - drive
        do = hp - 0.08 * hz - drive
        dg = hp - 0.02 * hz - drive
        solved = c["md_o"] * do
        pair = -(rock * bo) - c["mo_o"] * do
        gas_water = -(rock * rs * bo) - solved
        rows = (
            a0 + c["mw_p"] * dw + mw + well * c["mw"],
            rock * bw + c["mw_s"] * dw,
            jnp.zeros_like(p),
            a3 + c["mo_p"] * do + mo + well * c["mo"],
            pair,
            pair,
            a6 + c["mg_p"] * dg + c["md_p"] * do + mgd + well * (c["mg"] + c["md"]),
            gas_water,
            rock * bg + c["mg_s"] * dg + gas_water,
        )
        for e in range(9):
            diag_ref[e, i] = rows[e].astype(BF16)
        rhs = -(r0 + r1 + r2)
        rhs_ref[i] = rhs
        pd_ref[i] = pd
        first_ref[i] = rhs / pd
        return carry

    lax.fori_loop(0, 16, finish, 0)
    out_copy.wait()


def update_kernel(
    first_ref, rhs_ref, pd_ref, cond_ref, condlow_ref, fcond_ref, fc_ref, fl_ref,
    out_ref,
    sbuf, rbuf, hsend, hrecv, ghl, acc, fs, fr, hs, hr,
):
    slots = fc_ref.shape[3]
    barrier, count = greet()
    hsend[0, 0] = first_ref[15]
    hsend[1, 0] = first_ref[0]
    hsend[2, 0] = first_ref[:, 15, :]
    hsend[3, 0] = first_ref[:, 0, :]
    counts = (1, 1, 1, 1)
    for k in range(4):
        there = neighbour(8 - SIDES[k])[0]

        @pl.when(jnp.logical_not(there))
        def _():
            hrecv[k] = jnp.zeros_like(hrecv[k])

    def clear(d):
        @pl.when(jnp.logical_not(neighbour(d)[0]))
        def _():
            rbuf[d] = jnp.zeros_like(rbuf[d])

    eight(clear)
    hi, lo = split(as_rows(first_ref[...]))
    ghl[0:128, :] = hi
    ghl[128:256, :] = lo
    pl.semaphore_wait(barrier, count)
    for k in range(4):
        pl.when(neighbour(SIDES[k])[0])(halo_copy(hsend, hrecv, k, 1, hs, hr).start)

    def gather(d):
        di, dj = d // 3, d % 3
        for c in range(0, slots, CHUNK):
            column = fc_ref[0, di, pl.ds(dj, 1), pl.ds(c, CHUNK)]
            layer = fl_ref[0, di, pl.ds(dj, 1), pl.ds(c, CHUNK)]
            row, lane = cell_rows(column, layer)
            lines = jnp.dot(ghl[...], hot_ones(hot(lane, 256)), preferred_element_type=F32)
            mask = lax.broadcasted_iota(jnp.int32, (128, CHUNK), 0) == row
            sbuf[d, :, pl.ds(c, CHUNK)] = jnp.sum(
                jnp.where(mask, lines[0:128] + lines[128:256], 0.0), axis=0, keepdims=True
            )
        pl.when(neighbour(d)[0])(fault_copy(sbuf, rbuf, d, fs, fr, 8 - d).start)

    eight(gather)
    acc[...] = jnp.zeros_like(acc)
    wait_halos(hsend, hrecv, counts, hs, hr)
    wait_faults(sbuf, rbuf, fs, fr)

    def scatter(d):
        di, dj = d // 3, d % 3
        for c in range(0, slots, CHUNK):
            column = fc_ref[0, di, pl.ds(dj, 1), pl.ds(c, CHUNK)]
            layer = fl_ref[0, di, pl.ds(dj, 1), pl.ds(c, CHUNK)]
            row, lane = cell_rows(column, layer)
            value = fcond_ref[di, pl.ds(dj, 1), pl.ds(c, CHUNK)] * rbuf[d, :, pl.ds(c, CHUNK)]
            acc[...] += lax.dot_general(
                jnp.concatenate(hot_values(hot(row, 128), value), axis=0),
                hot_ones(hot(lane, 256)),
                (((1,), (1,)), ((), ())),
                preferred_element_type=F32,
            )

    eight(scatter)
    row_id = lax.broadcasted_iota(jnp.int32, (16, 128), 0)

    def finish(i, carry):
        own = first_ref[i]
        before, after = jnp.maximum(i - 1, 0), jnp.minimum(i + 1, 15)
        up = jnp.where(i == 15, hrecv[1, 0], first_ref[after])
        down = jnp.where(i == 0, hrecv[0, 0], first_ref[before])
        total = cond_ref[0, i] * up
        total += jnp.where(i == 0, condlow_ref[0], cond_ref[0, before]) * down
        cj = cond_ref[1, i]
        up = jnp.where(row_id == 15, hrecv[3, 0, pl.ds(i, 1), :], pltpu.roll(own, 15, 0))
        down = jnp.where(row_id == 0, hrecv[2, 0, pl.ds(i, 1), :], pltpu.roll(own, 1, 0))
        cj_low = jnp.where(row_id == 0, condlow_ref[1, pl.ds(i, 1), :], pltpu.roll(cj, 1, 0))
        total += cj * up + cj_low * down
        ck = cond_ref[2, i]
        total += ck * pltpu.roll(own, 127, 1) + pltpu.roll(ck * own, 1, 1)
        at = pl.multiple_of(i * 8, 8)
        fault = acc[pl.ds(at, 8), :] + acc[pl.ds(at + 128, 8), :]
        total += jnp.concatenate([fault[:, 0:128], fault[:, 128:256]], axis=0)
        out_ref[i] = (rhs_ref[i] + total) / pd_ref[i]
        return carry

    lax.fori_loop(0, 16, finish, 0)


def vmem(count):
    return [pl.BlockSpec(memory_space=pltpu.VMEM)] * count


def per_device(p, sw, sg, z, pv, om, t, fc, fl, ft, pc, wi, wp):
    slots = fc.shape[3]
    block = jax.ShapeDtypeStruct(p.shape, F32)
    dma = pltpu.SemaphoreType.DMA
    near, far, halo = pl.pallas_call(
        exchange_kernel,
        out_shape=[
            jax.ShapeDtypeStruct((4, 3, 3, slots), F32),
            jax.ShapeDtypeStruct((4, 3, 3, slots), F32),
            jax.ShapeDtypeStruct((4, 5, 16, 128), F32),
        ],
        in_specs=vmem(7),
        out_specs=vmem(3),
        scratch_shapes=[
            pltpu.VMEM((9, 4, slots), F32),
            pltpu.VMEM((9, 4, slots), F32),
            pltpu.VMEM((4, 5, 16, 128), F32),
            pltpu.VMEM((4, 5, 16, 128), F32),
            pltpu.VMEM((512, 256), BF16),
            pltpu.VMEM((512, 256), BF16),
            dma((9,)),
            dma((9,)),
            dma((4,)),
            dma((4,)),
        ],
        compiler_params=pltpu.CompilerParams(
            collective_id=0, has_side_effects=True, vmem_limit_bytes=VMEM_BYTES
        ),
        name="exchange",
    )(p, sw, sg, z, t, fc, fl)
    res, diag, face, fault, first, rhs, pd, cond, condlow, fcond = pl.pallas_call(
        terms_kernel,
        out_shape=[
            jax.ShapeDtypeStruct((3, 16, 16, 128), F32),
            jax.ShapeDtypeStruct((9, 16, 16, 128), BF16),
            jax.ShapeDtypeStruct((3, 2, 9, 16, 16, 128), BF16),
            jax.ShapeDtypeStruct((9, 1, 3, 3, slots), BF16),
            block,
            block,
            block,
            jax.ShapeDtypeStruct((3, 16, 16, 128), F32),
            jax.ShapeDtypeStruct((2, 16, 128), F32),
            jax.ShapeDtypeStruct((3, 3, slots), F32),
        ],
        in_specs=vmem(16),
        out_specs=vmem(2) + [pl.BlockSpec(memory_space=pl.ANY)] + vmem(7),
        scratch_shapes=[
            pltpu.VMEM((3, 2, 9, 16, 16, 128), BF16),
            pltpu.VMEM((1024, 256), F32),
            pltpu.VMEM((256, 256), F32),
            pltpu.VMEM((8, 16, 128), F32),
            pltpu.VMEM((8, 3, 3, slots), F32),
            dma,
        ],
        compiler_params=pltpu.CompilerParams(vmem_limit_bytes=VMEM_BYTES),
        name="terms",
    )(p, sw, sg, z, pv, om, t, fc, fl, ft, pc, wi, wp, near, far, halo)
    update = pl.pallas_call(
        update_kernel,
        out_shape=block,
        in_specs=vmem(8),
        out_specs=vmem(1)[0],
        scratch_shapes=[
            pltpu.VMEM((9, 1, slots), F32),
            pltpu.VMEM((9, 1, slots), F32),
            pltpu.VMEM((4, 1, 16, 128), F32),
            pltpu.VMEM((4, 1, 16, 128), F32),
            pltpu.VMEM((256, 256), BF16),
            pltpu.VMEM((256, 256), F32),
            dma((9,)),
            dma((9,)),
            dma((4,)),
            dma((4,)),
        ],
        compiler_params=pltpu.CompilerParams(
            collective_id=1, has_side_effects=True, vmem_limit_bytes=VMEM_BYTES
        ),
        name="update",
    )(first, rhs, pd, cond, condlow, fcond, fc, fl)
    return res, diag, face, fault, update


def solution(mesh):
    cells = P("col", "row", None)
    stacked = P(None, "col", "row", None)
    owned = P(("col", "row"), None, None, None)
    wells = P(("col", "row"), None)
    return jax.shard_map(
        per_device,
        mesh=mesh,
        in_specs=(cells,) * 5 + (stacked,) * 2 + (owned,) * 3 + (wells,) * 3,
        out_specs=(
            stacked,
            stacked,
            P(None, None, None, "col", "row", None),
            P(None, ("col", "row"), None, None, None),
            cells,
        ),
        check_vma=False,
    )
```

profile of v0, /device:TPU:27, one launch (start us, length us, event | category | flops | bytes accessed | tf_op | source)
XLA Modules:
  0.0 54.6 jit_solution(15315261240547631711)
XLA Ops:
  0.6 0.8 %copy.20.fc_ref = s32[1,3,3,1024]{3,2,1,0:T(4,128)S(1)} copy(s32[1,3,3,1024]{3,0,2,1:T(1,128)} %param.20) | data formatting | bytes 73728 | tf_op args[7]
  1.4 0.8 %copy.21.fl_ref = s32[1,3,3,1024]{3,2,1,0:T(4,128)S(1)} copy(s32[1,3,3,1024]{3,0,2,1:T(1,128)} %param.21) | data formatting | bytes 73728 | tf_op args[8]
  2.2 0.8 %copy.22.ft_ref = f32[1,3,3,1024]{3,2,1,0:T(4,128)S(1)} copy(f32[1,3,3,1024]{3,0,2,1:T(1,128)} %param.22) | data formatting | bytes 73728 | tf_op args[9]
  3.0 0.0 copy-start
  3.0 1.0 %copy-done = f32[3,16,16,128]{3,2,1,0:T(8,128)S(1)} copy-done((f32[3,16,16,128]{3,2,1,0:T(8,128)S(1)}, f32[3,16,16,128]{3,2,1,0:T(8,128)}, u32[]{:S(2)}) %copy-start) | copy-done | bytes 393240
  4.0 0.0 copy-start.1
  4.0 0.9 %copy-done.1 = f32[16,16,128]{2,1,0:T(8,128)S(1)} copy-done((f32[16,16,128]{2,1,0:T(8,128)S(1)}, f32[16,16,128]{2,1,0:T(8,128)}, u32[]{:S(2)}) %copy-start.1) | copy-done | bytes 131096
  4.9 0.0 copy-start.2
  4.9 0.9 %copy-done.2 = f32[16,16,128]{2,1,0:T(8,128)S(1)} copy-done((f32[16,16,128]{2,1,0:T(8,128)S(1)}, f32[16,16,128]{2,1,0:T(8,128)}, u32[]{:S(2)}) %copy-start.2) | copy-done | bytes 131096
  5.8 0.0 copy-start.3
  5.8 0.9 %copy-done.3 = f32[16,16,128]{2,1,0:T(8,128)S(1)} copy-done((f32[16,16,128]{2,1,0:T(8,128)S(1)}, f32[16,16,128]{2,1,0:T(8,128)}, u32[]{:S(2)}) %copy-start.3) | copy-done | bytes 131096
  6.7 0.0 copy-start.4
  6.7 0.9 %copy-done.4 = f32[16,16,128]{2,1,0:T(8,128)S(1)} copy-done((f32[16,16,128]{2,1,0:T(8,128)S(1)}, f32[16,16,128]{2,1,0:T(8,128)}, u32[]{:S(2)}) %copy-start.4) | copy-done | bytes 131096
  7.6 13.5 %exchange.1 = (f32[4,3,3,1024]{3,2,1,0:T(4,128)S(1)}, f32[4,3,3,1024]{3,2,1,0:T(4,128)S(1)}, f32[4,5,16,128]{3,2,1,0:T(8,128)S(1)}) custom-call(f32[16,16,128]{2,1,0:T(8,128)S(1)} %copy-done.1, f32[16,16,128]{2,1,0:T(8,128)S(1)} %copy-done.2, f32[16,16,128]{2,1,0:T(8,128)S(1)} %copy-done.3, f32[16,16,128]{2,1,0:T(8,128)S(1)} %copy-done.4, ...), custom_call_target="tpu_custom_call" | custom-call | tf_op jit(solution)/shard_map/exchange/pallas_call | solution.py:537
  21.1 0.0 copy-start.5
  21.1 1.0 %copy-done.5 = f32[3,16,16,128]{3,2,1,0:T(8,128)S(1)} copy-done((f32[3,16,16,128]{3,2,1,0:T(8,128)S(1)}, f32[3,16,16,128]{3,2,1,0:T(8,128)}, u32[]{:S(2)}) %copy-start.5) | copy-done | bytes 393240
  22.1 0.0 copy-start.6
  22.1 0.9 %copy-done.6 = f32[16,16,128]{2,1,0:T(8,128)S(1)} copy-done((f32[16,16,128]{2,1,0:T(8,128)S(1)}, f32[16,16,128]{2,1,0:T(8,128)}, u32[]{:S(2)}) %copy-start.6) | copy-done | bytes 131096
  23.0 0.0 copy-start.7
  23.0 0.7 %copy-done.7 = s32[1,128]{1,0:T(1,128)S(1)} copy-done((s32[1,128]{1,0:T(1,128)S(1)}, s32[1,128]{1,0:T(1,128)}, u32[]{:S(2)}) %copy-start.7) | copy-done | bytes 536
  23.7 0.0 copy-start.8
  23.7 0.7 %copy-done.8 = f32[1,128]{1,0:T(1,128)S(1)} copy-done((f32[1,128]{1,0:T(1,128)S(1)}, f32[1,128]{1,0:T(1,128)}, u32[]{:S(2)}) %copy-start.8) | copy-done | bytes 536
  24.3 0.0 copy-start.9
  24.3 0.7 %copy-done.9 = f32[1,128]{1,0:T(1,128)S(1)} copy-done((f32[1,128]{1,0:T(1,128)S(1)}, f32[1,128]{1,0:T(1,128)}, u32[]{:S(2)}) %copy-start.9) | copy-done | bytes 536
  25.0 15.5 %terms.1 = (f32[3,16,16,128]{3,2,1,0:T(8,128)}, bf16[9,16,16,128]{3,2,1,0:T(8,128)(2,1)}, bf16[3,2,9,16,16,128]{5,4,3,2,1,0:T(8,128)(2,1)}, bf16[9,1,3,3,1024]{4...) custom-call(f32[16,16,128]{2,1,0:T(8,128)S(1)} %copy-done.1, ...), custom_call_target="tpu_custom_call" | custom-call | tf_op jit(solution)/shard_map/terms/pallas_call | solution.py:563
  40.5 13.4 %update.1 = f32[16,16,128]{2,1,0:T(8,128)S(1)} custom-call(f32[16,16,128]{2,1,0:T(8,128)S(1)} %get-tuple-element.25.first_ref, f32[16,16,128]{2,1,0:T(8,128)S(1)} %get-tuple-element.26.rhs_ref, f32[16,16,128]{2,1,0:T(8,128)S(1)} %get-tuple-element.27.pd_ref, f32[3,16,16,128]{3,2,1,0:T(8,128)S(1)} %get-tuple-element.28.cond_ref, ...), custom_call_target="tpu_custom_call" | custom-call | tf_op jit(solution)/shard_map/update/pallas_call | solution.py:590
  54.0 0.7 %copy.26 = f32[16,16,128]{2,1,0:T(8,128)} copy(f32[16,16,128]{2,1,0:T(8,128)S(1)} %update.1) | data formatting | bytes 262144
Async XLA Ops:
  3.0 1.0 %copy-start = (f32[3,16,16,128]{3,2,1,0:T(8,128)S(1)}, f32[3,16,16,128]{3,2,1,0:T(8,128)}, u32[]{:S(2)}) copy-start(f32[3,16,16,128]{3,2,1,0:T(8,128)} %t_ref.3) | copy-start | bytes 1179652
  4.0 0.9 %copy-start.1 = (f32[16,16,128]{2,1,0:T(8,128)S(1)}, f32[16,16,128]{2,1,0:T(8,128)}, u32[]{:S(2)}) copy-start(f32[16,16,128]{2,1,0:T(8,128)} %p_ref.3) | copy-start | bytes 393220
  4.9 0.9 %copy-start.2 = (f32[16,16,128]{2,1,0:T(8,128)S(1)}, f32[16,16,128]{2,1,0:T(8,128)}, u32[]{:S(2)}) copy-start(f32[16,16,128]{2,1,0:T(8,128)} %sw_ref.3) | copy-start | bytes 393220
  5.8 0.9 %copy-start.3 = (f32[16,16,128]{2,1,0:T(8,128)S(1)}, f32[16,16,128]{2,1,0:T(8,128)}, u32[]{:S(2)}) copy-start(f32[16,16,128]{2,1,0:T(8,128)} %sg_ref.3) | copy-start | bytes 393220
  6.7 0.9 %copy-start.4 = (f32[16,16,128]{2,1,0:T(8,128)S(1)}, f32[16,16,128]{2,1,0:T(8,128)}, u32[]{:S(2)}) copy-start(f32[16,16,128]{2,1,0:T(8,128)} %z_ref.3) | copy-start | bytes 393220
  21.1 1.0 %copy-start.5 = (f32[3,16,16,128]{3,2,1,0:T(8,128)S(1)}, f32[3,16,16,128]{3,2,1,0:T(8,128)}, u32[]{:S(2)}) copy-start(f32[3,16,16,128]{3,2,1,0:T(8,128)} %om_ref.1) | copy-start | bytes 1179652
  22.1 0.9 %copy-start.6 = (f32[16,16,128]{2,1,0:T(8,128)S(1)}, f32[16,16,128]{2,1,0:T(8,128)}, u32[]{:S(2)}) copy-start(f32[16,16,128]{2,1,0:T(8,128)} %pv_ref.1) | copy-start | bytes 393220
  23.0 0.7 %copy-start.7 = (s32[1,128]{1,0:T(1,128)S(1)}, s32[1,128]{1,0:T(1,128)}, u32[]{:S(2)}) copy-start(s32[1,128]{1,0:T(1,128)} %pc_ref.1) | copy-start | bytes 1540
  23.7 0.7 %copy-start.8 = (f32[1,128]{1,0:T(1,128)S(1)}, f32[1,128]{1,0:T(1,128)}, u32[]{:S(2)}) copy-start(f32[1,128]{1,0:T(1,128)} %wi_ref.1) | copy-start | bytes 1540
  24.3 0.7 %copy-start.9 = (f32[1,128]{1,0:T(1,128)S(1)}, f32[1,128]{1,0:T(1,128)}, u32[]{:S(2)}) copy-start(f32[1,128]{1,0:T(1,128)} %wp_ref.1) | copy-start | bytes 1540
where the time goes:
time: 55.1 us; the launch traced here: 54.6 us
  Pallas kernels  42.4 us (77%)
  local copies, waits for them, and re-layouts  11.5 us (21%)
  between operations  0.69 us (1%)
    pallas_call x1, Pallas kernels, per_device(): pl.pallas_call(terms_kernel, out_shape=[jax.ShapeDtypeStruct((3, 16, 16,...  15.5 us
    pallas_call x1, Pallas kernels, per_device(): pl.pallas_call(exchange_kernel, out_shape=[jax.ShapeDtypeStruct((4, 3, 3,...  13.5 us
    pallas_call x1, Pallas kernels, per_device(): pl.pallas_call(update_kernel, out_shape=block, in_specs=vmem(8), out_spec...  13.4 us
    unnamed x24, local copies, waits for them, and re-layouts  11.5 us

commit v1 on v0

v1 whole, which is shorter than its diff:
```python
import jax
import jax.numpy as jnp
from jax import lax
from jax.experimental import pallas as pl
from jax.experimental.pallas import tpu as pltpu
from jax.sharding import PartitionSpec as P

F32 = jnp.float32
BF16 = jnp.bfloat16
MESH = pl.DeviceIdType.MESH
VMEM_BYTES = 40 * 1024 * 1024


def split(x):
    hi = x.astype(BF16)
    return hi, (x - hi.astype(F32)).astype(BF16)


def cell_terms(p, sw, sg):
    oil = 1.0 - sw - sg
    bw = 1.0 + 0.05 * p
    bo = 1.0 + 0.1 * p
    bg = 1.0 + 0.4 * p
    rs = 0.5 + 0.2 * p
    w2 = sw * (sw * (1.0 / 0.3))
    o2 = oil * (oil * (1.0 / 0.8))
    g2 = sg * (sg * (1.0 / 0.05))
    mo = bo * o2
    mo_p = 0.1 * o2
    mo_o = bo * (oil * (2.0 / 0.8))
    return dict(
        mw=bw * w2,
        mo=mo,
        mg=bg * g2,
        md=rs * mo,
        mw_p=0.05 * w2,
        mw_s=bw * (sw * (2.0 / 0.3)),
        mo_p=mo_p,
        mo_o=mo_o,
        mg_p=0.4 * g2,
        mg_s=bg * (sg * (2.0 / 0.05)),
        md_p=0.2 * mo + rs * mo_p,
        md_o=rs * mo_o,
    )


def face_terms(t, a, b, pa, pb, za, zb):
    half = 0.5 * t
    hp = half * (pa - pb)
    hz = half * (za - zb)
    ww = hp - 0.1 * hz
    wo = hp - 0.08 * hz
    wg = hp - 0.02 * hz
    sum_w = a["mw"] + b["mw"]
    sum_o = a["mo"] + b["mo"]
    sum_g = a["mg"] + b["mg"]
    sum_d = a["md"] + b["md"]
    mw = half * sum_w
    mo = half * sum_o
    mgd = half * (sum_g + sum_d)
    flux = (sum_w * ww, sum_o * wo, sum_g * wg + sum_d * wo)
    return (hp, hz, mw, mo, mgd) + flux, (ww, wo, wg)


def block_rows(c, ww, wo, wg, mw, mo, mgd):
    oil = c["mo_o"] * wo
    solved = c["md_o"] * wo
    zero = jnp.zeros_like(ww)
    return (
        c["mw_p"] * ww + mw,
        c["mw_s"] * ww,
        zero,
        c["mo_p"] * wo + mo,
        -oil,
        -oil,
        c["mg_p"] * wg + c["md_p"] * wo + mgd,
        -solved,
        c["mg_s"] * wg - solved,
    )


def neighbour(d):
    a, b = lax.axis_index("col"), lax.axis_index("row")
    ta, tb = a + d // 3 - 1, b + d % 3 - 1
    na, nb = lax.axis_size("col"), lax.axis_size("row")
    there = (ta >= 0) & (ta < na) & (tb >= 0) & (tb < nb)
    return there, (ta, tb)


def group(g):
    return [jnp.where(g == 0, (0, 2, 6, 8)[e], 2 * e + 1) for e in range(4)]


def two_groups(body):
    def step(g, carry):
        body(group(g))
        return carry

    lax.fori_loop(0, 2, step, 0)


SIDES = (7, 1, 5, 3)


def greet():
    barrier = pltpu.get_barrier_semaphore()
    count = 0
    for d in (0, 1, 2, 3, 5, 6, 7, 8):
        there, target = neighbour(d)

        @pl.when(there)
        def _():
            pl.semaphore_signal(barrier, inc=1, device_id=target, device_id_type=MESH)

        count = count + there.astype(jnp.int32)
    return barrier, count


def halo_copy(src, dst, k, count, send_sem, recv_sem):
    return pltpu.make_async_remote_copy(
        src_ref=src.at[k, pl.ds(0, count)],
        dst_ref=dst.at[k, pl.ds(0, count)],
        send_sem=send_sem.at[k],
        recv_sem=recv_sem.at[k],
        device_id=neighbour(SIDES[k])[1],
        device_id_type=MESH,
    )


def fault_copy(src, dst, d, send_sem, recv_sem, back):
    return pltpu.make_async_remote_copy(
        src_ref=src.at[d],
        dst_ref=dst.at[back],
        send_sem=send_sem.at[d],
        recv_sem=recv_sem.at[back],
        device_id=neighbour(d)[1],
        device_id_type=MESH,
    )


def wait_halos(src, dst, counts, send_sem, recv_sem):
    for k in range(4):
        copy = halo_copy(src, dst, k, counts[k], send_sem, recv_sem)
        pl.when(neighbour(SIDES[k])[0])(copy.wait_send)
        pl.when(neighbour(8 - SIDES[k])[0])(copy.wait_recv)


def send_group(src, dst, ds, send_sem, recv_sem):
    for d in ds:
        pl.when(neighbour(d)[0])(fault_copy(src, dst, d, send_sem, recv_sem, 8 - d).start)


def wait_group(src, dst, ds, send_sem, recv_sem):
    for d in ds:
        copy = fault_copy(src, dst, d, send_sem, recv_sem, d)

        @pl.when(neighbour(d)[0])
        def _():
            copy.wait_send()
            copy.wait_recv()


def clear_missing(hrecv, rbuf):
    for k in range(4):

        @pl.when(jnp.logical_not(neighbour(8 - SIDES[k])[0]))
        def _():
            hrecv[k] = jnp.zeros_like(hrecv[k])

    def one(d, carry):
        @pl.when(jnp.logical_not(neighbour(d)[0]) | (d == 4))
        def _():
            rbuf[d] = jnp.zeros_like(rbuf[d])

        return carry

    lax.fori_loop(0, 9, one, 0)


def cell_rows(column, layer):
    return (column >> 4) * 8 + (column & 7), ((column >> 3) & 1) * 128 + layer


def hot(index, size):
    slots = index.shape[1]
    row = jnp.broadcast_to(index.astype(F32), (16, slots)).astype(BF16)
    iota = lax.broadcasted_iota(jnp.int32, (size, slots), 0).astype(F32).astype(BF16)
    return iota.reshape(size // 16, 16, slots) == row[None]


def hot_values(mask, value_row):
    slots = value_row.shape[1]
    hi, lo = split(jnp.broadcast_to(value_row, (16, slots)))
    zero = jnp.zeros((), BF16)
    return [jnp.where(mask, v[None], zero).reshape(128, slots) for v in (hi, lo)]


def hot_ones(mask):
    size = mask.shape[0] * 16
    return jnp.where(mask, jnp.ones((), BF16), jnp.zeros((), BF16)).reshape(size, mask.shape[2])


def lanes(parts):
    return jnp.concatenate(parts, axis=1)


def rows(parts):
    return jnp.concatenate(parts, axis=0)


def as_rows(x):
    return lanes([x[:, 0:8, :].reshape(128, 128), x[:, 8:16, :].reshape(128, 128)])


def dot_slots(weighted, put):
    return lax.dot_general(weighted, put, (((1,), (1,)), ((), ())), preferred_element_type=F32)


def gather(pieces, count, row_ref, lane_ref, d, store):
    for c in range(0, 8, 2):
        pick = lanes([hot_ones(hot(lane_ref[d, pl.ds(q, 1), :], 256)) for q in (c, c + 1)])
        lines = None
        for piece in pieces:
            line = jnp.dot(piece, pick, preferred_element_type=F32)
            lines = line if lines is None else lines + line
        for s in range(2):
            mask = lax.broadcasted_iota(jnp.int32, (128, 128), 0) == row_ref[d, pl.ds(c + s, 1), :]
            for f in range(count):
                part = lines[f * 128 : (f + 1) * 128, s * 128 : (s + 1) * 128]
                if len(pieces) == 1:
                    at = (count + f) * 128
                    part = part + lines[at : at + 128, s * 128 : (s + 1) * 128]
                store(f, c + s, jnp.sum(jnp.where(mask, part, 0.0), axis=0, keepdims=True))


def lower_side(values):
    return (-values[0], -values[1], values[2], values[3], values[4]) + tuple(-v for v in values[5:])


def exchange_kernel(
    p_hbm, sw_hbm, sg_hbm, z_hbm, t_hbm, fc_hbm, fl_hbm, ft_hbm,
    near_ref, far_ref, row_ref, lane_ref, ft_ref, blocks, acc, cond_ref, condlow_ref,
    x_ref, t_ref, fc_ref, fl_ref, sbuf, rbuf, hsend, hrecv, ghi, glo, lowj, in_sem, fs, fr, hs, hr,
):
    barrier, count = greet()
    loads = [pltpu.make_async_copy(fc_hbm, fc_ref, in_sem.at[0]), pltpu.make_async_copy(fl_hbm, fl_ref, in_sem.at[1])]
    for f, ref in enumerate((p_hbm, sw_hbm, sg_hbm, z_hbm)):
        loads.append(pltpu.make_async_copy(ref, x_ref.at[f], in_sem.at[2 + f]))
    loads.append(pltpu.make_async_copy(t_hbm, t_ref, in_sem.at[6]))
    loads.append(pltpu.make_async_copy(ft_hbm, ft_ref, in_sem.at[7]))
    for load in loads:
        load.start()
    clear_missing(hrecv, rbuf)
    sbuf[4] = jnp.zeros_like(sbuf[4])
    for load in loads[:2]:
        load.wait()
    row, lane = cell_rows(fc_ref[...], fl_ref[...])
    row_ref[...] = row
    lane_ref[...] = lane
    for load in loads[2:]:
        load.wait()
    for f in range(4):
        hsend[0, f] = x_ref[f, 15]
        hsend[1, f] = x_ref[f, 0]
        hsend[2, f] = x_ref[f, :, 15, :]
        hsend[3, f] = x_ref[f, :, 0, :]
    hsend[0, 4] = t_ref[0, 15]
    hsend[2, 4] = t_ref[1, :, 15, :]
    counts = (5, 4, 5, 4)
    for f in range(4):
        hi, lo = split(as_rows(x_ref[f]))
        ghi[pl.ds(f * 128, 128), :] = hi
        glo[pl.ds(f * 128, 128), :] = lo
    pl.semaphore_wait(barrier, count)
    for k in range(4):
        pl.when(neighbour(SIDES[k])[0])(halo_copy(hsend, hrecv, k, counts[k], hs, hr).start)

    def gather_group(ds):
        for d in ds:

            def store(f, q, value):
                sbuf[d, f, pl.ds(q, 1), :] = value

            gather([ghi[...], glo[...]], 4, row_ref, lane_ref, d, store)
        send_group(sbuf, rbuf, ds, fs, fr)

    two_groups(gather_group)
    wait_halos(hsend, hrecv, counts, hs, hr)

    def low_face(k, fields):
        a = [hrecv[k, f] for f in range(4)]
        values, _ = face_terms(
            hrecv[k, 4], cell_terms(*a[:3]), cell_terms(*fields[:3]), a[0], fields[0], a[3], fields[3]
        )
        condlow_ref[k // 2] = values[2] + values[3] + values[4]
        return lower_side(values)

    for v, value in enumerate(low_face(2, [x_ref[f, :, 0, :] for f in range(4)])):
        lowj[v] = value
    carry = low_face(0, [x_ref[f, 0] for f in range(4)])
    row_id = lax.broadcasted_iota(jnp.int32, (16, 128), 0)
    lane_id = lax.broadcasted_iota(jnp.int32, (16, 128), 1)
    keep_i = jnp.where(neighbour(SIDES[0])[0], 1.0, 0.0)
    keep_j = jnp.where(neighbour(SIDES[2])[0], 1.0, 0.0)

    def plane(i, carry):
        own = [x_ref[f, i] for f in range(4)]
        a = cell_terms(*own[:3])
        last = i == 15
        after = jnp.minimum(i + 1, 15)
        total = list(carry)
        out_carry = None
        for n in range(3):
            t = t_ref[n, i]
            if n == 0:
                nxt = [jnp.where(last, hrecv[1, f], x_ref[f, after]) for f in range(4)]
                t = t * jnp.where(last, keep_i, 1.0)
            elif n == 1:
                nxt = [
                    jnp.where(row_id == 15, hrecv[3, f, pl.ds(i, 1), :], pltpu.roll(own[f], 15, 0))
                    for f in range(4)
                ]
                t = jnp.where(row_id == 15, t * keep_j, t)
            else:
                nxt = [pltpu.roll(own[f], 127, 1) for f in range(4)]
                t = jnp.where(lane_id == 127, 0.0, t)
            b = cell_terms(*nxt[:3])
            values, (ww, wo, wg) = face_terms(t, a, b, own[0], nxt[0], own[3], nxt[3])
            mw, mo, mgd = values[2:5]
            cond_ref[n, i] = mw + mo + mgd
            upper = block_rows(b, ww, wo, wg, -mw, -mo, -mgd)
            lower = block_rows(a, -ww, -wo, -wg, -mw, -mo, -mgd)
            for e in range(9):
                blocks[n, 0, e, i] = upper[e].astype(BF16)
                blocks[n, 1, e, i] = lower[e].astype(BF16)
            total = [x + y for x, y in zip(total, values)]
            below = lower_side(values)
            if n == 0:
                out_carry = below
            elif n == 1:
                for v in range(8):
                    shifted = jnp.where(row_id == 0, lowj[v, pl.ds(i, 1), :], pltpu.roll(below[v], 1, 0))
                    total[v] = total[v] + shifted
            else:
                total = [x + pltpu.roll(y, 1, 1) for x, y in zip(total, below)]
        for v in range(8):
            at = pl.multiple_of(v * 128 + i * 8, 8)
            acc[pl.ds(at, 8), 0:128] = total[v][0:8]
            acc[pl.ds(at, 8), 128:256] = total[v][8:16]
        return tuple(out_carry)

    lax.fori_loop(0, 16, plane, tuple(carry))
    two_groups(lambda ds: wait_group(sbuf, rbuf, ds, fs, fr))
    near_ref[...] = sbuf[...]
    far_ref[...] = rbuf[...]


def terms_kernel(
    near_ref, far_ref, row_ref, lane_ref, ft_ref, blocks, face_acc,
    p_hbm, sw_hbm, sg_hbm, pv_hbm, om_hbm, pc_hbm, wi_hbm, wp_hbm,
    res_ref, diag_ref, face_hbm, fault_ref, first_ref, rhs_ref, pd_ref, fcond_ref,
    x_ref, om_ref, w_ref, pc_ref, acc, wacc, chan, fault_rows, in_sem, out_sem,
):
    out_copy = pltpu.make_async_copy(blocks, face_hbm, out_sem)
    loads = [pltpu.make_async_copy(pc_hbm, pc_ref, in_sem.at[0]), pltpu.make_async_copy(om_hbm, om_ref, in_sem.at[1])]
    for f, ref in enumerate((p_hbm, sw_hbm, sg_hbm, pv_hbm)):
        loads.append(pltpu.make_async_copy(ref, x_ref.at[f], in_sem.at[2 + f]))
    for f, ref in enumerate((wi_hbm, wp_hbm)):
        loads.append(pltpu.make_async_copy(ref, w_ref.at[f], in_sem.at[6 + f]))
    for load in loads:
        load.start()
    out_copy.start()

    near = [near_ref[:, f].reshape(72, 128) for f in range(4)]
    far = [far_ref[:, f].reshape(72, 128) for f in range(4)]
    a, b = cell_terms(*near[:3]), cell_terms(*far[:3])
    values, (ww, wo, wg) = face_terms(
        ft_ref[...].reshape(72, 128), a, b, near[0], far[0], near[3], far[3]
    )
    mw, mo, mgd = values[2:5]
    fcond_ref[...] = (mw + mo + mgd).reshape(9, 8, 128)
    for v in range(8):
        chan[v] = values[v].reshape(9, 8, 128)
    for e, value in enumerate(block_rows(b, ww, wo, wg, -mw, -mo, -mgd)):
        fault_rows[e] = value
    acc[...] = face_acc[...]

    def scatter_group(ds):
        for d in ds:
            for c in range(0, 8, 2):
                pair = (c, c + 1)
                put = lanes([hot_ones(hot(lane_ref[d, pl.ds(q, 1), :], 256)) for q in pair])
                masks = [hot(row_ref[d, pl.ds(q, 1), :], 128) for q in pair]
                his, los = [], []
                for v in range(8):
                    both = [hot_values(m, chan[v, d, pl.ds(q, 1), :]) for m, q in zip(masks, pair)]
                    his.append(lanes([x[0] for x in both]))
                    los.append(lanes([x[1] for x in both]))
                acc[...] += dot_slots(lanes([rows(his), rows(los)]), lanes([put, put]))

    two_groups(scatter_group)

    def fault_out(e, carry):
        for di in range(3):
            for q in range(8):
                line = fault_rows[e, pl.ds(di * 24 + q, 3, 8), :]
                fault_ref[e, 0, di, :, pl.ds(q * 128, 128)] = line.astype(BF16)
        return carry

    lax.fori_loop(0, 9, fault_out, 0)
    for load in loads:
        load.wait()
    cell = pc_ref[...]
    row, lane = cell_rows(cell >> 7, cell & 127)
    mask = hot(row, 128)
    hi_w, lo_w = hot_values(mask, w_ref[0])
    hi_q, lo_q = hot_values(mask, w_ref[0] * w_ref[1])
    put = hot_ones(hot(lane, 256))
    wacc[...] = dot_slots(lanes([rows([hi_w, hi_q]), rows([lo_w, lo_q])]), lanes([put, put]))

    def rows_of(ref, start):
        at = pl.multiple_of(start, 8)
        return rows([ref[pl.ds(at, 8), 0:128], ref[pl.ds(at, 8), 128:256]])

    def finish(i, carry):
        p, sw, sg = x_ref[0, i], x_ref[1, i], x_ref[2, i]
        c = cell_terms(p, sw, sg)
        hp, hz, mw, mo, mgd, rw, ro, rg = [rows_of(acc, v * 128 + i * 8) for v in range(8)]
        well = rows_of(wacc, i * 8)
        drive = rows_of(wacc, 128 + i * 8) - p * well
        oil = 1.0 - sw - sg
        pv = x_ref[3, i]
        rock = 2.0 * (pv * (1.0 + 0.02 * p))
        rock_p = 0.04 * pv
        bw, bo, bg, rs = 1.0 + 0.05 * p, 1.0 + 0.1 * p, 1.0 + 0.4 * p, 0.5 + 0.2 * p
        ob = oil * bo
        gas = sg * bg + rs * ob
        r0 = rock * sw * bw - 2.0 * om_ref[0, i] + rw - drive * c["mw"]
        r1 = rock * ob - 2.0 * om_ref[1, i] + ro - drive * c["mo"]
        r2 = rock * gas - 2.0 * om_ref[2, i] + rg - drive * (c["mg"] + c["md"])
        res_ref[0, i], res_ref[1, i], res_ref[2, i] = r0, r1, r2
        a0 = rock_p * sw * bw + rock * sw * 0.05
        a3 = rock_p * ob + rock * oil * 0.1
        a6 = rock_p * gas + rock * (0.4 * sg + 0.2 * ob + 0.1 * rs * oil)
        total = c["mw"] + c["mo"] + c["mg"] + c["md"]
        pd = a0 + a3 + a6 + mw + mo + mgd + well * total
        dw = hp - 0.1 * hz - drive
        do = hp - 0.08 * hz - drive
        dg = hp - 0.02 * hz - drive
        solved = c["md_o"] * do
        pair = -(rock * bo) - c["mo_o"] * do
        gas_water = -(rock * rs * bo) - solved
        out = (
            a0 + c["mw_p"] * dw + mw + well * c["mw"],
            rock * bw + c["mw_s"] * dw,
            jnp.zeros_like(p),
            a3 + c["mo_p"] * do + mo + well * c["mo"],
            pair,
            pair,
            a6 + c["mg_p"] * dg + c["md_p"] * do + mgd + well * (c["mg"] + c["md"]),
            gas_water,
            rock * bg + c["mg_s"] * dg + gas_water,
        )
        for e in range(9):
            diag_ref[e, i] = out[e].astype(BF16)
        rhs = -(r0 + r1 + r2)
        rhs_ref[i] = rhs
        pd_ref[i] = pd
        first_ref[i] = rhs / pd
        return carry

    lax.fori_loop(0, 16, finish, 0)
    out_copy.wait()


def update_kernel(
    first_ref, rhs_ref, pd_ref, cond_ref, condlow_ref, fcond_ref, row_ref, lane_ref,
    out_ref,
    sbuf, rbuf, hsend, hrecv, ghl, acc, fs, fr, hs, hr,
):
    barrier, count = greet()
    hsend[0, 0] = first_ref[15]
    hsend[1, 0] = first_ref[0]
    hsend[2, 0] = first_ref[:, 15, :]
    hsend[3, 0] = first_ref[:, 0, :]
    counts = (1, 1, 1, 1)
    clear_missing(hrecv, rbuf)
    hi, lo = split(as_rows(first_ref[...]))
    ghl[0:128, :] = hi
    ghl[128:256, :] = lo
    pl.semaphore_wait(barrier, count)
    for k in range(4):
        pl.when(neighbour(SIDES[k])[0])(halo_copy(hsend, hrecv, k, 1, hs, hr).start)

    def gather_group(ds):
        for d in ds:

            def store(f, q, value):
                sbuf[d, pl.ds(q, 1), :] = value

            gather([ghl[...]], 1, row_ref, lane_ref, d, store)
        send_group(sbuf, rbuf, ds, fs, fr)

    two_groups(gather_group)
    wait_halos(hsend, hrecv, counts, hs, hr)
    row_id = lax.broadcasted_iota(jnp.int32, (16, 128), 0)

    def faces(i, carry):
        own = first_ref[i]
        before, after = jnp.maximum(i - 1, 0), jnp.minimum(i + 1, 15)
        up = jnp.where(i == 15, hrecv[1, 0], first_ref[after])
        down = jnp.where(i == 0, hrecv[0, 0], first_ref[before])
        total = cond_ref[0, i] * up
        total += jnp.where(i == 0, condlow_ref[0], cond_ref[0, before]) * down
        cj = cond_ref[1, i]
        up = jnp.where(row_id == 15, hrecv[3, 0, pl.ds(i, 1), :], pltpu.roll(own, 15, 0))
        down = jnp.where(row_id == 0, hrecv[2, 0, pl.ds(i, 1), :], pltpu.roll(own, 1, 0))
        cj_low = jnp.where(row_id == 0, condlow_ref[1, pl.ds(i, 1), :], pltpu.roll(cj, 1, 0))
        total += cj * up + cj_low * down
        ck = cond_ref[2, i]
        total += ck * pltpu.roll(own, 127, 1) + pltpu.roll(ck * own, 1, 1)
        at = pl.multiple_of(i * 8, 8)
        acc[pl.ds(at, 8), 0:128] = total[0:8]
        acc[pl.ds(at, 8), 128:256] = total[8:16]
        return carry

    lax.fori_loop(0, 16, faces, 0)
    acc[128:256, :] = jnp.zeros((128, 256), F32)

    def scatter_group(ds):
        wait_group(sbuf, rbuf, ds, fs, fr)
        for d in ds:
            values = fcond_ref[d] * rbuf[d]
            for c in range(0, 8, 2):
                pair = (c, c + 1)
                put = lanes([hot_ones(hot(lane_ref[d, pl.ds(q, 1), :], 256)) for q in pair])
                both = [
                    hot_values(hot(row_ref[d, pl.ds(q, 1), :], 128), values[q : q + 1]) for q in pair
                ]
                weighted = rows([lanes([x[0] for x in both]), lanes([x[1] for x in both])])
                acc[...] += dot_slots(weighted, put)

    two_groups(scatter_group)

    def finish(i, carry):
        at = pl.multiple_of(i * 8, 8)
        total = acc[pl.ds(at, 8), :] + acc[pl.ds(at + 128, 8), :]
        total = rows([total[:, 0:128], total[:, 128:256]])
        out_ref[i] = (rhs_ref[i] + total) / pd_ref[i]
        return carry

    lax.fori_loop(0, 16, finish, 0)


def in_vmem(count):
    return [pl.BlockSpec(memory_space=pltpu.VMEM)] * count


def in_hbm(count):
    return [pl.BlockSpec(memory_space=pltpu.HBM)] * count


def per_device(p, sw, sg, z, pv, om, t, fc, fl, ft, pc, wi, wp):
    def dense(x):
        return jnp.transpose(x, (1, 2, 0, 3)).reshape(9, 8, 128)

    def f32(*shape):
        return jax.ShapeDtypeStruct(shape, F32)

    slots = fc.shape[3]
    cells = p.shape
    fc, fl, ft = dense(fc), dense(fl), dense(ft)
    p, sw, sg, z, pv, om, t, fc, fl, ft, pc, wi, wp = [
        pltpu.with_memory_space_constraint(x, pltpu.HBM)
        for x in (p, sw, sg, z, pv, om, t, fc, fl, ft, pc, wi, wp)
    ]
    dma = pltpu.SemaphoreType.DMA
    index = jax.ShapeDtypeStruct((9, 8, 128), jnp.int32)
    near, far, row, lane, ft_dense, blocks, acc, cond, condlow = pl.pallas_call(
        exchange_kernel,
        out_shape=[
            f32(9, 4, 8, 128),
            f32(9, 4, 8, 128),
            index,
            index,
            f32(9, 8, 128),
            jax.ShapeDtypeStruct((3, 2, 9) + cells, BF16),
            f32(1024, 256),
            f32(3, *cells),
            f32(2, 16, 128),
        ],
        in_specs=in_hbm(8),
        out_specs=in_vmem(9),
        scratch_shapes=[
            pltpu.VMEM((4,) + cells, F32),
            pltpu.VMEM((3,) + cells, F32),
            pltpu.VMEM((9, 8, 128), jnp.int32),
            pltpu.VMEM((9, 8, 128), jnp.int32),
            pltpu.VMEM((9, 4, 8, 128), F32),
            pltpu.VMEM((9, 4, 8, 128), F32),
            pltpu.VMEM((4, 5, 16, 128), F32),
            pltpu.VMEM((4, 5, 16, 128), F32),
            pltpu.VMEM((512, 256), BF16),
            pltpu.VMEM((512, 256), BF16),
            pltpu.VMEM((8, 16, 128), F32),
            dma((8,)),
            dma((9,)),
            dma((9,)),
            dma((4,)),
            dma((4,)),
        ],
        compiler_params=pltpu.CompilerParams(
            collective_id=0, has_side_effects=True, vmem_limit_bytes=VMEM_BYTES
        ),
        name="exchange",
    )(p, sw, sg, z, t, fc, fl, ft)
    res, diag, face, fault, first, rhs, pd, fcond = pl.pallas_call(
        terms_kernel,
        out_shape=[
            f32(3, *cells),
            jax.ShapeDtypeStruct((9,) + cells, BF16),
            jax.ShapeDtypeStruct((3, 2, 9) + cells, BF16),
            jax.ShapeDtypeStruct((9, 1, 3, 3, slots), BF16),
            f32(*cells),
            f32(*cells),
            f32(*cells),
            f32(9, 8, 128),
        ],
        in_specs=in_vmem(7) + in_hbm(8),
        out_specs=in_vmem(2) + in_hbm(1) + in_vmem(5),
        scratch_shapes=[
            pltpu.VMEM((4,) + cells, F32),
            pltpu.VMEM((3,) + cells, F32),
            pltpu.VMEM((2, 1, 128), F32),
            pltpu.VMEM((1, 128), jnp.int32),
            pltpu.VMEM((1024, 256), F32),
            pltpu.VMEM((256, 256), F32),
            pltpu.VMEM((8, 9, 8, 128), F32),
            pltpu.VMEM((9, 72, 128), F32),
            dma((8,)),
            dma,
        ],
        compiler_params=pltpu.CompilerParams(vmem_limit_bytes=VMEM_BYTES),
        name="terms",
    )(near, far, row, lane, ft_dense, blocks, acc, p, sw, sg, pv, om, pc, wi, wp)
    update = pl.pallas_call(
        update_kernel,
        out_shape=f32(*cells),
        in_specs=in_vmem(8),
        out_specs=in_vmem(1)[0],
        scratch_shapes=[
            pltpu.VMEM((9, 8, 128), F32),
            pltpu.VMEM((9, 8, 128), F32),
            pltpu.VMEM((4, 1, 16, 128), F32),
            pltpu.VMEM((4, 1, 16, 128), F32),
            pltpu.VMEM((256, 256), BF16),
            pltpu.VMEM((256, 256), F32),
            dma((9,)),
            dma((9,)),
            dma((4,)),
            dma((4,)),
        ],
        compiler_params=pltpu.CompilerParams(
            collective_id=1, has_side_effects=True, vmem_limit_bytes=VMEM_BYTES
        ),
        name="update",
    )(first, rhs, pd, cond, condlow, fcond, row, lane)
    return res, diag, face, fault, update


def solution(mesh):
    cells = P("col", "row", None)
    stacked = P(None, "col", "row", None)
    owned = P(("col", "row"), None, None, None)
    wells = P(("col", "row"), None)
    return jax.shard_map(
        per_device,
        mesh=mesh,
        in_specs=(cells,) * 5 + (stacked,) * 2 + (owned,) * 3 + (wells,) * 3,
        out_specs=(
            stacked,
            stacked,
            P(None, None, None, "col", "row", None),
            P(None, ("col", "row"), None, None, None),
            cells,
        ),
        check_vma=False,
    )
```

time: 55.1 us -> 35.7 us (0.65)
  local copies, waits for them, and re-layouts: 11.5 us -> 0.66 us
  Pallas kernels: 42.4 us -> 33.8 us
    unnamed x24 -> x1, local copies, waits for them, and re-layouts: 11.5 us -> 0.66 us
    pallas_call x3, Pallas kernels: 42.4 us -> 33.8 us  [the longest x1 12.7 us: per_device(): pl.pallas_call(exchange_kernel, out_shape=[f32(9, 4, 8, 128), f32(9, 4, 8...]
where the time goes in v1:
time: 35.7 us; the launch traced here: 35.2 us
  Pallas kernels  33.8 us (95%)
  local copies, waits for them, and re-layouts  0.66 us (2%)
  between operations  0.66 us (2%)
    pallas_call x1, Pallas kernels, per_device(): pl.pallas_call(exchange_kernel, out_shape=[f32(9, 4, 8, 128), f32(9, 4, 8...  12.7 us
    pallas_call x1, Pallas kernels, per_device(): pl.pallas_call(terms_kernel, out_shape=[f32(3, *cells), jax.ShapeDtypeStr...  11.6 us
    pallas_call x1, Pallas kernels, per_device(): pl.pallas_call(update_kernel, out_shape=f32(*cells), in_specs=in_vmem(8),...  9.55 us

profile of v1, /device:TPU:27, one launch (start us, length us, event | category | flops | bytes accessed | tf_op | source)
XLA Modules:
  0.0 35.2 jit_solution(3393559554641287468)
XLA Ops:
  0.6 12.7 %exchange.1 = (f32[9,4,8,128]{3,2,1,0:T(8,128)S(1)}, f32[9,4,8,128]{3,2,1,0:T(8,128)S(1)}, s32[9,8,128]{2,1,0:T(8,128)S(1)}, s32[9,8,128]{2,1,0:T(8,128)S(1)}, f...) custom-call(f32[16,16,128]{2,1,0:T(8,128)} %p_hbm.3, ...), custom_call_target="tpu_custom_call" | custom-call | tf_op jit(solution)/shard_map/exchange/pallas_call | solution.py:579
  13.3 11.6 %terms.1 = (f32[3,16,16,128]{3,2,1,0:T(8,128)}, bf16[9,16,16,128]{3,2,1,0:T(8,128)(2,1)}, bf16[3,2,9,16,16,128]{5,4,3,2,1,0:T(8,128)(2,1)}, bf16[9,1,3,3,1024]{4...) custom-call(f32[9,4,8,128]{3,2,1,0:T(8,128)S(1)} %get-tuple-element., ...), custom_call_target="tpu_custom_call" | custom-call | tf_op jit(solution)/shard_map/terms/pallas_call | solution.py:617
  24.9 9.5 %update.1 = f32[16,16,128]{2,1,0:T(8,128)S(1)} custom-call(f32[16,16,128]{2,1,0:T(8,128)S(1)} %get-tuple-element.33.first_ref, f32[16,16,128]{2,1,0:T(8,128)S(1)} %get-tuple-element.34.rhs_ref, f32[16,16,128]{2,1,0:T(8,128)S(1)} %get-tuple-element.35.pd_ref, f32[3,16,16,128]{3,2,1,0:T(8,128)S(1)} %get-tuple-element.36.cond_ref, ...), custom_call_target="tpu_custom_call" | custom-call | tf_op jit(solution)/shard_map/update/pallas_call | solution.py:646
  34.5 0.7 %copy.19 = f32[16,16,128]{2,1,0:T(8,128)} copy(f32[16,16,128]{2,1,0:T(8,128)S(1)} %update.1) | data formatting | bytes 262144

commit v2 on v1

v2 whole, which is shorter than its diff:
```python
import jax
import jax.numpy as jnp
from jax import lax
from jax.experimental import pallas as pl
from jax.experimental.pallas import tpu as pltpu
from jax.sharding import PartitionSpec as P

F32 = jnp.float32
BF16 = jnp.bfloat16
MESH = pl.DeviceIdType.MESH
VMEM_BYTES = 40 * 1024 * 1024


def split(x):
    hi = x.astype(BF16)
    return hi, (x - hi.astype(F32)).astype(BF16)


def cell_terms(p, sw, sg):
    oil = 1.0 - sw - sg
    bw = 1.0 + 0.05 * p
    bo = 1.0 + 0.1 * p
    bg = 1.0 + 0.4 * p
    rs = 0.5 + 0.2 * p
    w2 = sw * (sw * (1.0 / 0.3))
    o2 = oil * (oil * (1.0 / 0.8))
    g2 = sg * (sg * (1.0 / 0.05))
    mo = bo * o2
    mo_p = 0.1 * o2
    mo_o = bo * (oil * (2.0 / 0.8))
    return dict(
        mw=bw * w2,
        mo=mo,
        mg=bg * g2,
        md=rs * mo,
        mw_p=0.05 * w2,
        mw_s=bw * (sw * (2.0 / 0.3)),
        mo_p=mo_p,
        mo_o=mo_o,
        mg_p=0.4 * g2,
        mg_s=bg * (sg * (2.0 / 0.05)),
        md_p=0.2 * mo + rs * mo_p,
        md_o=rs * mo_o,
    )


def face_terms(t, a, b, pa, pb, za, zb):
    half = 0.5 * t
    hp = half * (pa - pb)
    hz = half * (za - zb)
    ww = hp - 0.1 * hz
    wo = hp - 0.08 * hz
    wg = hp - 0.02 * hz
    sum_w = a["mw"] + b["mw"]
    sum_o = a["mo"] + b["mo"]
    sum_g = a["mg"] + b["mg"]
    sum_d = a["md"] + b["md"]
    mw = half * sum_w
    mo = half * sum_o
    mgd = half * (sum_g + sum_d)
    flux = (sum_w * ww, sum_o * wo, sum_g * wg + sum_d * wo)
    return (hp, hz, mw, mo, mgd) + flux, (ww, wo, wg)


def block_rows(c, ww, wo, wg, mw, mo, mgd):
    oil = c["mo_o"] * wo
    solved = c["md_o"] * wo
    zero = jnp.zeros_like(ww)
    return (
        c["mw_p"] * ww + mw,
        c["mw_s"] * ww,
        zero,
        c["mo_p"] * wo + mo,
        -oil,
        -oil,
        c["mg_p"] * wg + c["md_p"] * wo + mgd,
        -solved,
        c["mg_s"] * wg - solved,
    )


def neighbour(d):
    a, b = lax.axis_index("col"), lax.axis_index("row")
    ta, tb = a + d // 3 - 1, b + d % 3 - 1
    na, nb = lax.axis_size("col"), lax.axis_size("row")
    there = (ta >= 0) & (ta < na) & (tb >= 0) & (tb < nb)
    return there, (ta, tb)


def direction(g, h, u):
    return jnp.where(g == 0, 2 * u + 6 * h, 4 * h + 2 * u + 1)


def group(g):
    return [direction(g, h, u) for h in range(2) for u in range(2)]


def two_groups(body):
    def step(g, carry):
        body(group(g))
        return carry

    lax.fori_loop(0, 2, step, 0)


SIDES = (7, 1, 5, 3)


def greet():
    barrier = pltpu.get_barrier_semaphore()
    count = 0
    for d in (0, 1, 2, 3, 5, 6, 7, 8):
        there, target = neighbour(d)

        @pl.when(there)
        def _():
            pl.semaphore_signal(barrier, inc=1, device_id=target, device_id_type=MESH)

        count = count + there.astype(jnp.int32)
    return barrier, count


def halo_copy(src, dst, k, count, send_sem, recv_sem):
    return pltpu.make_async_remote_copy(
        src_ref=src.at[k, pl.ds(0, count)],
        dst_ref=dst.at[k, pl.ds(0, count)],
        send_sem=send_sem.at[k],
        recv_sem=recv_sem.at[k],
        device_id=neighbour(SIDES[k])[1],
        device_id_type=MESH,
    )


def fault_copy(src, dst, d, send_sem, recv_sem, back):
    return pltpu.make_async_remote_copy(
        src_ref=src.at[d],
        dst_ref=dst.at[back],
        send_sem=send_sem.at[d],
        recv_sem=recv_sem.at[back],
        device_id=neighbour(d)[1],
        device_id_type=MESH,
    )


def wait_halos(src, dst, counts, send_sem, recv_sem):
    for k in range(4):
        copy = halo_copy(src, dst, k, counts[k], send_sem, recv_sem)
        pl.when(neighbour(SIDES[k])[0])(copy.wait_send)
        pl.when(neighbour(8 - SIDES[k])[0])(copy.wait_recv)


def send_group(src, dst, ds, send_sem, recv_sem):
    for d in ds:
        pl.when(neighbour(d)[0])(fault_copy(src, dst, d, send_sem, recv_sem, 8 - d).start)


def wait_group(src, dst, ds, send_sem, recv_sem):
    for d in ds:
        copy = fault_copy(src, dst, d, send_sem, recv_sem, d)

        @pl.when(neighbour(d)[0])
        def _():
            copy.wait_send()
            copy.wait_recv()


def clear_missing(hrecv, rbuf):
    for k in range(4):

        @pl.when(jnp.logical_not(neighbour(8 - SIDES[k])[0]))
        def _():
            hrecv[k] = jnp.zeros_like(hrecv[k])

    def one(d, carry):
        @pl.when(jnp.logical_not(neighbour(d)[0]) | (d == 4))
        def _():
            rbuf[d] = jnp.zeros_like(rbuf[d])

        return carry

    lax.fori_loop(0, 9, one, 0)


def cell_rows(column, layer):
    return (column >> 4) * 8 + (column & 7), ((column >> 3) & 1) * 128 + layer


def hot(index, size):
    slots = index.shape[1]
    row = jnp.broadcast_to(index.astype(F32), (16, slots)).astype(BF16)
    iota = lax.broadcasted_iota(jnp.int32, (size, slots), 0).astype(F32).astype(BF16)
    return iota.reshape(size // 16, 16, slots) == row[None]


def hot_values(mask, value_row):
    slots = value_row.shape[1]
    hi, lo = split(jnp.broadcast_to(value_row, (16, slots)))
    zero = jnp.zeros((), BF16)
    return [jnp.where(mask, v[None], zero).reshape(128, slots) for v in (hi, lo)]


def hot_ones(mask):
    size = mask.shape[0] * 16
    return jnp.where(mask, jnp.ones((), BF16), jnp.zeros((), BF16)).reshape(size, mask.shape[2])


def lanes(parts):
    return jnp.concatenate(parts, axis=1)


def rows(parts):
    return jnp.concatenate(parts, axis=0)


def as_rows(x):
    return lanes([x[:, 0:8, :].reshape(128, 128), x[:, 8:16, :].reshape(128, 128)])


def dot_slots(weighted, put):
    return lax.dot_general(weighted, put, (((1,), (1,)), ((), ())), preferred_element_type=F32)


def gather(pieces, count, row_ref, lane_ref, d, store):
    for c in range(0, 8, 2):
        pick = lanes([hot_ones(hot(lane_ref[d, pl.ds(q, 1), :], 256)) for q in (c, c + 1)])
        lines = None
        for piece in pieces:
            line = jnp.dot(piece, pick, preferred_element_type=F32)
            lines = line if lines is None else lines + line
        for s in range(2):
            mask = lax.broadcasted_iota(jnp.int32, (128, 128), 0) == row_ref[d, pl.ds(c + s, 1), :]
            for f in range(count):
                part = lines[f * 128 : (f + 1) * 128, s * 128 : (s + 1) * 128]
                if len(pieces) == 1:
                    at = (count + f) * 128
                    part = part + lines[at : at + 128, s * 128 : (s + 1) * 128]
                store(f, c + s, jnp.sum(jnp.where(mask, part, 0.0), axis=0, keepdims=True))


def lower_side(values):
    return (-values[0], -values[1], values[2], values[3], values[4]) + tuple(-v for v in values[5:])


def plane_loop(body):
    def step(i, carry):
        body(2 * i)
        body(2 * i + 1)
        return carry

    lax.fori_loop(0, 8, step, 0)


def rows_of(ref, start):
    at = pl.multiple_of(start, 8)
    return rows([ref[pl.ds(at, 8), 0:128], ref[pl.ds(at, 8), 128:256]])


def scatter_first(ds, row_ref, lane_ref, fcond_ref, far_ref, acc2):
    for d in ds:
        values = fcond_ref[d] * far_ref[d]
        for c in range(0, 8, 2):
            pair = (c, c + 1)
            put = lanes([hot_ones(hot(lane_ref[d, pl.ds(q, 1), :], 256)) for q in pair])
            both = [hot_values(hot(row_ref[d, pl.ds(q, 1), :], 128), values[q : q + 1]) for q in pair]
            weighted = rows([lanes([x[0] for x in both]), lanes([x[1] for x in both])])
            acc2[...] += dot_slots(weighted, put)


def system_kernel(
    p_hbm, sw_hbm, sg_hbm, z_hbm, pv_hbm, om_hbm, t_hbm, fc_hbm, fl_hbm, ft_hbm, pc_hbm, wi_hbm, wp_hbm,
    blocks, res_ref, diag_ref, fault_ref, rhs_ref, pd_ref, acc2, far2, fcond_ref, row_ref, lane_ref,
    x_ref, t_ref, om_ref, fc_ref, fl_ref, ft_ref, pc_ref, w_ref, sbuf, rbuf, hsend, hrecv, ghi, glo, lowj,
    carry_ref, acc, fa, wacc, chan, fault_rows, cond_ref, condlow_ref, first_ref, sbuf2, rbuf2, hsend2, hrecv2, ghl,
    in_sem, fs, fr, hs, hr, fs2, fr2, hs2, hr2,
):
    barrier, count = greet()
    pairs = [(fc_hbm, fc_ref), (fl_hbm, fl_ref)]
    pairs += [(ref, x_ref.at[f]) for f, ref in enumerate((p_hbm, sw_hbm, sg_hbm, z_hbm))]
    pairs += [(t_hbm, t_ref), (ft_hbm, ft_ref), (pc_hbm, pc_ref), (wi_hbm, w_ref.at[0]), (wp_hbm, w_ref.at[1])]
    pairs += [(pv_hbm, x_ref.at[4]), (om_hbm, om_ref)]
    loads = [pltpu.make_async_copy(a, b, in_sem.at[n]) for n, (a, b) in enumerate(pairs)]
    for load in loads:
        load.start()
    clear_missing(hrecv, rbuf)
    clear_missing(hrecv2, rbuf2)
    fault_rows[:, 32:40, :] = jnp.zeros((9, 8, 128), F32)
    fcond_ref[4] = jnp.zeros((8, 128), F32)
    acc[...] = jnp.zeros_like(acc)
    for load in loads[:2]:
        load.wait()
    row, lane = cell_rows(fc_ref[...], fl_ref[...])
    row_ref[...] = row
    lane_ref[...] = lane
    for load in loads[2:7]:
        load.wait()
    for f in range(4):
        hsend[0, f] = x_ref[f, 15]
        hsend[1, f] = x_ref[f, 0]
        hsend[2, f] = x_ref[f, :, 15, :]
        hsend[3, f] = x_ref[f, :, 0, :]
    hsend[0, 4] = t_ref[0, 15]
    hsend[2, 4] = t_ref[1, :, 15, :]
    counts = (5, 4, 5, 4)
    for f in range(4):
        hi, lo = split(as_rows(x_ref[f]))
        ghi[pl.ds(f * 128, 128), :] = hi
        glo[pl.ds(f * 128, 128), :] = lo
    pl.semaphore_wait(barrier, count)
    for k in range(4):
        pl.when(neighbour(SIDES[k])[0])(halo_copy(hsend, hrecv, k, counts[k], hs, hr).start)

    def gather_group(ds):
        for d in ds:

            def store(f, q, value):
                sbuf[d, f, pl.ds(q, 1), :] = value

            gather([ghi[...], glo[...]], 4, row_ref, lane_ref, d, store)
        send_group(sbuf, rbuf, ds, fs, fr)

    two_groups(gather_group)
    for load in loads[7:]:
        load.wait()
    wait_halos(hsend, hrecv, counts, hs, hr)

    def low_face(k, fields):
        a = [hrecv[k, f] for f in range(4)]
        values, _ = face_terms(
            hrecv[k, 4], cell_terms(*a[:3]), cell_terms(*fields[:3]), a[0], fields[0], a[3], fields[3]
        )
        condlow_ref[k // 2] = values[2] + values[3] + values[4]
        return lower_side(values)

    for v, value in enumerate(low_face(2, [x_ref[f, :, 0, :] for f in range(4)])):
        lowj[v] = value
    for v, value in enumerate(low_face(0, [x_ref[f, 0] for f in range(4)])):
        carry_ref[v] = value
    row_id = lax.broadcasted_iota(jnp.int32, (16, 128), 0)
    lane_id = lax.broadcasted_iota(jnp.int32, (16, 128), 1)
    keep_i = jnp.where(neighbour(SIDES[0])[0], 1.0, 0.0)
    keep_j = jnp.where(neighbour(SIDES[2])[0], 1.0, 0.0)

    def plane(i, carry):
        own = [x_ref[f, i] for f in range(4)]
        a = cell_terms(*own[:3])
        last = i == 15
        after = jnp.minimum(i + 1, 15)
        total = list(carry)
        out_carry = None
        for n in range(3):
            t = t_ref[n, i]
            if n == 0:
                nxt = [jnp.where(last, hrecv[1, f], x_ref[f, after]) for f in range(4)]
                t = t * jnp.where(last, keep_i, 1.0)
            elif n == 1:
                nxt = [
                    jnp.where(row_id == 15, hrecv[3, f, pl.ds(i, 1), :], pltpu.roll(own[f], 15, 0))
                    for f in range(4)
                ]
                t = jnp.where(row_id == 15, t * keep_j, t)
            else:
                nxt = [pltpu.roll(own[f], 127, 1) for f in range(4)]
                t = jnp.where(lane_id == 127, 0.0, t)
            b = cell_terms(*nxt[:3])
            values, (ww, wo, wg) = face_terms(t, a, b, own[0], nxt[0], own[3], nxt[3])
            mw, mo, mgd = values[2:5]
            cond_ref[n, i] = mw + mo + mgd
            upper = block_rows(b, ww, wo, wg, -mw, -mo, -mgd)
            lower = block_rows(a, -ww, -wo, -wg, -mw, -mo, -mgd)
            for e in range(9):
                blocks[n, 0, e, i] = upper[e].astype(BF16)
                blocks[n, 1, e, i] = lower[e].astype(BF16)
            total = [x + y for x, y in zip(total, values)]
            below = lower_side(values)
            if n == 0:
                out_carry = below
            elif n == 1:
                for v in range(8):
                    shifted = jnp.where(row_id == 0, lowj[v, pl.ds(i, 1), :], pltpu.roll(below[v], 1, 0))
                    total[v] = total[v] + shifted
            else:
                total = [x + pltpu.roll(y, 1, 1) for x, y in zip(total, below)]
        for v in range(8):
            fa[v, i] = total[v]
        return out_carry

    def fault_terms(d):
        near = [sbuf[d, f] for f in range(4)]
        far = [rbuf[d, f] for f in range(4)]
        a, b = cell_terms(*near[:3]), cell_terms(*far[:3])
        values, (ww, wo, wg) = face_terms(ft_ref[d], a, b, near[0], far[0], near[3], far[3])
        mw, mo, mgd = values[2:5]
        fcond_ref[d] = mw + mo + mgd
        for v in range(8):
            chan[v, d] = values[v]
        for e, value in enumerate(block_rows(b, ww, wo, wg, -mw, -mo, -mgd)):
            fault_rows[e, pl.ds(pl.multiple_of(d * 8, 8), 8), :] = value

    def scatter(d, c):
        pair = (c, c + 1)
        put = lanes([hot_ones(hot(lane_ref[d, pl.ds(q, 1), :], 256)) for q in pair])
        masks = [hot(row_ref[d, pl.ds(q, 1), :], 128) for q in pair]
        his, los = [], []
        for v in range(8):
            both = [hot_values(m, chan[v, d, pl.ds(q, 1), :]) for m, q in zip(masks, pair)]
            his.append(lanes([x[0] for x in both]))
            los.append(lanes([x[1] for x in both]))
        acc[...] += dot_slots(lanes([rows(his), rows(los)]), lanes([put, put]))

    def main_group(g, carry):
        wait_group(sbuf, rbuf, group(g), fs, fr)
        for d in group(g):
            fault_terms(d)

        def half(h, carry):
            below = [carry_ref[v] for v in range(8)]
            for u in range(2):
                for m in range(2):
                    for c in (4 * m, 4 * m + 2):
                        scatter(direction(g, h, u), c)
                    below = plane(g * 8 + h * 4 + u * 2 + m, below)
            for v in range(8):
                carry_ref[v] = below[v]
            return carry

        lax.fori_loop(0, 2, half, 0)
        return carry

    lax.fori_loop(0, 2, main_group, 0)

    cell = pc_ref[...]
    row, lane = cell_rows(cell >> 7, cell & 127)
    mask = hot(row, 128)
    hi_w, lo_w = hot_values(mask, w_ref[0])
    hi_q, lo_q = hot_values(mask, w_ref[0] * w_ref[1])
    put = hot_ones(hot(lane, 256))
    wacc[...] = dot_slots(lanes([rows([hi_w, hi_q]), rows([lo_w, lo_q])]), lanes([put, put]))

    def sums(i):
        return [fa[v, i] + rows_of(acc, v * 128 + i * 8) for v in range(8)]

    def accumulation(i):
        p, sw, sg = x_ref[0, i], x_ref[1, i], x_ref[2, i]
        well = rows_of(wacc, i * 8)
        drive = rows_of(wacc, 128 + i * 8) - p * well
        oil = 1.0 - sw - sg
        pv = x_ref[4, i]
        rock = 2.0 * (pv * (1.0 + 0.02 * p))
        rock_p = 0.04 * pv
        bw, bo, bg, rs = 1.0 + 0.05 * p, 1.0 + 0.1 * p, 1.0 + 0.4 * p, 0.5 + 0.2 * p
        ob = oil * bo
        gas = sg * bg + rs * ob
        a0 = rock_p * sw * bw + rock * sw * 0.05
        a3 = rock_p * ob + rock * oil * 0.1
        a6 = rock_p * gas + rock * (0.4 * sg + 0.2 * ob + 0.1 * rs * oil)
        return cell_terms(p, sw, sg), well, drive, rock, (rock * sw * bw, rock * ob, rock * gas), (a0, a3, a6), (bw, bo, bg, rs)

    def residuals(i):
        _, _, mw, mo, mgd, rw, ro, rg = sums(i)
        c, well, drive, rock, held, slope, _ = accumulation(i)
        r0 = held[0] - 2.0 * om_ref[0, i] + rw - drive * c["mw"]
        r1 = held[1] - 2.0 * om_ref[1, i] + ro - drive * c["mo"]
        r2 = held[2] - 2.0 * om_ref[2, i] + rg - drive * (c["mg"] + c["md"])
        res_ref[0, i], res_ref[1, i], res_ref[2, i] = r0, r1, r2
        total = c["mw"] + c["mo"] + c["mg"] + c["md"]
        pd = slope[0] + slope[1] + slope[2] + mw + mo + mgd + well * total
        rhs = -(r0 + r1 + r2)
        rhs_ref[i] = rhs
        pd_ref[i] = pd
        first_ref[i] = rhs / pd

    def diagonals(i):
        hp, hz, mw, mo, mgd, _, _, _ = sums(i)
        c, well, drive, rock, held, slope, (bw, bo, bg, rs) = accumulation(i)
        dw = hp - 0.1 * hz - drive
        do = hp - 0.08 * hz - drive
        dg = hp - 0.02 * hz - drive
        pair = -(rock * bo) - c["mo_o"] * do
        gas_water = -(rock * rs * bo) - c["md_o"] * do
        out = (
            slope[0] + c["mw_p"] * dw + mw + well * c["mw"],
            rock * bw + c["mw_s"] * dw,
            jnp.zeros_like(dw),
            slope[1] + c["mo_p"] * do + mo + well * c["mo"],
            pair,
            pair,
            slope[2] + c["mg_p"] * dg + c["md_p"] * do + mgd + well * (c["mg"] + c["md"]),
            gas_water,
            rock * bg + c["mg_s"] * dg + gas_water,
        )
        for e in range(9):
            diag_ref[e, i] = out[e].astype(BF16)

    plane_loop(residuals)
    hsend2[0, 0] = first_ref[15]
    hsend2[1, 0] = first_ref[0]
    hsend2[2, 0] = first_ref[:, 15, :]
    hsend2[3, 0] = first_ref[:, 0, :]
    for k in range(4):
        pl.when(neighbour(SIDES[k])[0])(halo_copy(hsend2, hrecv2, k, 1, hs2, hr2).start)
    hi, lo = split(as_rows(first_ref[...]))
    ghl[0:128, :] = hi
    ghl[128:256, :] = lo

    def gather_first(ds):
        for d in ds:

            def store(f, q, value):
                sbuf2[d, pl.ds(q, 1), :] = value

            gather([ghl[...]], 1, row_ref, lane_ref, d, store)
        send_group(sbuf2, rbuf2, ds, fs2, fr2)

    two_groups(gather_first)

    def fault_out(e, carry):
        for di in range(3):
            for q in range(8):
                line = fault_rows[e, pl.ds(di * 24 + q, 3, 8), :]
                fault_ref[e, 0, di, :, pl.ds(q * 128, 128)] = line.astype(BF16)
        return carry

    lax.fori_loop(0, 9, fault_out, 0)
    plane_loop(diagonals)
    wait_halos(hsend2, hrecv2, (1, 1, 1, 1), hs2, hr2)

    def faces(i):
        own = first_ref[i]
        before, after = jnp.maximum(i - 1, 0), jnp.minimum(i + 1, 15)
        up = jnp.where(i == 15, hrecv2[1, 0], first_ref[after])
        down = jnp.where(i == 0, hrecv2[0, 0], first_ref[before])
        total = cond_ref[0, i] * up
        total += jnp.where(i == 0, condlow_ref[0], cond_ref[0, before]) * down
        cj = cond_ref[1, i]
        up = jnp.where(row_id == 15, hrecv2[3, 0, pl.ds(i, 1), :], pltpu.roll(own, 15, 0))
        down = jnp.where(row_id == 0, hrecv2[2, 0, pl.ds(i, 1), :], pltpu.roll(own, 1, 0))
        cj_low = jnp.where(row_id == 0, condlow_ref[1, pl.ds(i, 1), :], pltpu.roll(cj, 1, 0))
        total += cj * up + cj_low * down
        ck = cond_ref[2, i]
        total += ck * pltpu.roll(own, 127, 1) + pltpu.roll(ck * own, 1, 1)
        at = pl.multiple_of(i * 8, 8)
        acc2[pl.ds(at, 8), 0:128] = total[0:8]
        acc2[pl.ds(at, 8), 128:256] = total[8:16]

    plane_loop(faces)
    acc2[128:256, :] = jnp.zeros((128, 256), F32)
    wait_group(sbuf2, rbuf2, group(0), fs2, fr2)
    scatter_first(group(0), row_ref, lane_ref, fcond_ref, rbuf2, acc2)
    wait_group(sbuf2, rbuf2, group(1), fs2, fr2)
    far2[...] = rbuf2[...]


def write_kernel(
    blocks, res_ref, diag_ref, fault_ref, rhs_ref, pd_ref, acc_in, far2, fcond_ref, row_ref, lane_ref,
    face_hbm, res_hbm, diag_hbm, fault_hbm, out_hbm,
    acc2, out_ref, sem,
):
    pairs = ((blocks, face_hbm), (diag_ref, diag_hbm), (res_ref, res_hbm), (fault_ref, fault_hbm), (out_ref, out_hbm))
    copies = [pltpu.make_async_copy(a, b, sem.at[n]) for n, (a, b) in enumerate(pairs)]
    for copy in copies[:4]:
        copy.start()
    acc2[...] = acc_in[...]
    scatter_first((1, 3, 5, 7), row_ref, lane_ref, fcond_ref, far2, acc2)

    def finish(i):
        at = pl.multiple_of(i * 8, 8)
        total = acc2[pl.ds(at, 8), :] + acc2[pl.ds(at + 128, 8), :]
        total = rows([total[:, 0:128], total[:, 128:256]])
        out_ref[i] = (rhs_ref[i] + total) / pd_ref[i]

    plane_loop(finish)
    copies[4].start()
    for copy in copies:
        copy.wait()


def in_vmem(count):
    return [pl.BlockSpec(memory_space=pltpu.VMEM)] * count


def in_hbm(count):
    return [pl.BlockSpec(memory_space=pltpu.HBM)] * count


def per_device(*args):
    p, fc = args[0], args[7]
    slots, cells = fc.shape[3], p.shape

    def placed(n, x):
        if n in (7, 8, 9):
            x = jnp.transpose(x, (1, 2, 0, 3)).reshape(9, 8, 128)
        return pltpu.with_memory_space_constraint(x, pltpu.HBM)

    def f32(*shape):
        return jax.ShapeDtypeStruct(shape, F32)

    def scratch(*shape, dtype=F32):
        return pltpu.VMEM(shape, dtype)

    dma = pltpu.SemaphoreType.DMA
    index = jax.ShapeDtypeStruct((9, 8, 128), jnp.int32)
    face = jax.ShapeDtypeStruct((3, 2, 9) + cells, BF16)
    diag = jax.ShapeDtypeStruct((9,) + cells, BF16)
    fault = jax.ShapeDtypeStruct((9, 1, 3, 3, slots), BF16)
    held = pl.pallas_call(
        system_kernel,
        out_shape=[
            face,
            f32(3, *cells),
            diag,
            fault,
            f32(*cells),
            f32(*cells),
            f32(256, 256),
            f32(9, 8, 128),
            f32(9, 8, 128),
            index,
            index,
        ],
        in_specs=in_hbm(13),
        out_specs=in_vmem(11),
        scratch_shapes=[
            scratch(5, *cells),
            scratch(3, *cells),
            scratch(3, *cells),
            scratch(9, 8, 128, dtype=jnp.int32),
            scratch(9, 8, 128, dtype=jnp.int32),
            scratch(9, 8, 128),
            scratch(1, 128, dtype=jnp.int32),
            scratch(2, 1, 128),
            scratch(9, 4, 8, 128),
            scratch(9, 4, 8, 128),
            scratch(4, 5, 16, 128),
            scratch(4, 5, 16, 128),
            scratch(512, 256, dtype=BF16),
            scratch(512, 256, dtype=BF16),
            scratch(8, 16, 128),
            scratch(8, 16, 128),
            scratch(1024, 256),
            scratch(8, *cells),
            scratch(256, 256),
            scratch(8, 9, 8, 128),
            scratch(9, 72, 128),
            scratch(3, *cells),
            scratch(2, 16, 128),
            scratch(*cells),
            scratch(9, 8, 128),
            scratch(9, 8, 128),
            scratch(4, 1, 16, 128),
            scratch(4, 1, 16, 128),
            scratch(256, 256, dtype=BF16),
            dma((13,)),
            dma((9,)),
            dma((9,)),
            dma((4,)),
            dma((4,)),
            dma((9,)),
            dma((9,)),
            dma((4,)),
            dma((4,)),
        ],
        compiler_params=pltpu.CompilerParams(
            collective_id=0, has_side_effects=True, vmem_limit_bytes=VMEM_BYTES
        ),
        name="system",
    )(*[placed(n, x) for n, x in enumerate(args)])
    face, res, diag, fault, update = pl.pallas_call(
        write_kernel,
        out_shape=[face, f32(3, *cells), diag, fault, f32(*cells)],
        in_specs=in_vmem(11),
        out_specs=in_hbm(5),
        scratch_shapes=[scratch(256, 256), scratch(*cells), dma((5,))],
        compiler_params=pltpu.CompilerParams(vmem_limit_bytes=VMEM_BYTES),
        name="write",
    )(*held)
    return res, diag, face, fault, update


def solution(mesh):
    cells = P("col", "row", None)
    stacked = P(None, "col", "row", None)
    owned = P(("col", "row"), None, None, None)
    wells = P(("col", "row"), None)
    return jax.shard_map(
        per_device,
        mesh=mesh,
        in_specs=(cells,) * 5 + (stacked,) * 2 + (owned,) * 3 + (wells,) * 3,
        out_specs=(
            stacked,
            stacked,
            P(None, None, None, "col", "row", None),
            P(None, ("col", "row"), None, None, None),
            cells,
        ),
        check_vma=False,
    )
```

time: 35.7 us -> 31.9 us (0.89)
  Pallas kernels: 33.8 us -> 30.7 us
  local copies, waits for them, and re-layouts: 0.66 us -> 0 us
    pallas_call x3 -> x2, Pallas kernels: 33.8 us -> 30.7 us  [the longest x1 28.4 us: per_device(): pl.pallas_call(system_kernel, out_shape=[face, f32(3, *cells), diag, faul...]
    unnamed x1 -> x0, local copies, waits for them, and re-layouts: 0.66 us -> none
where the time goes in v2:
time: 31.9 us; the launch traced here: 31.3 us
  Pallas kernels  30.7 us (96%)
  between operations  0.64 us (2%)
    pallas_call x1, Pallas kernels, per_device(): pl.pallas_call(system_kernel, out_shape=[face, f32(3, *cells), diag, faul...  28.4 us
    pallas_call x1, Pallas kernels, per_device(): pl.pallas_call(write_kernel, out_shape=[face, f32(3, *cells), diag, fault...  2.26 us

profile of v2, /device:TPU:27, one launch (start us, length us, event | category | flops | bytes accessed | tf_op | source)
XLA Modules:
  0.0 31.3 jit_solution(5973984030814064940)
XLA Ops:
  0.6 28.4 %system.1 = (bf16[3,2,9,16,16,128]{5,4,3,2,1,0:T(8,128)(2,1)S(1)}, f32[3,16,16,128]{3,2,1,0:T(8,128)S(1)}, bf16[9,16,16,128]{3,2,1,0:T(8,128)(2,1)S(1)}, bf16[9,...) custom-call(f32[16,16,128]{2,1,0:T(8,128)} %p_hbm.1, ...), custom_call_target="tpu_custom_call" | custom-call | tf_op jit(solution)/shard_map/system/pallas_call | solution.py:605
  29.0 2.3 %write.1 = (bf16[3,2,9,16,16,128]{5,4,3,2,1,0:T(8,128)(2,1)}, f32[3,16,16,128]{3,2,1,0:T(8,128)}, bf16[9,16,16,128]{3,2,1,0:T(8,128)(2,1)}, bf16[9,1,3,3,1024]{4,3,2,1,0:T(4,128)(2,1)}, f32[16,16,128]{2,1,0:T(8,128)}) custom-call(bf16[3,2,9,16,16,128]{5,4,3,2,1,0:T(8,128)(2,1)S(1)} %get-tuple-element.21.blocks, ...), custom_call_target="tpu_custom_call" | custom-call | tf_op jit(solution)/shard_map/write/pallas_call | solution.py:667

commit v3 on v2

--- a/solution.py
+++ b/solution.py
@@ -7,6 +7,8 @@
 
 F32 = jnp.float32
 BF16 = jnp.bfloat16
+F8 = jnp.float8_e4m3fn
+LOW = 2.0**-6
 MESH = pl.DeviceIdType.MESH
 VMEM_BYTES = 40 * 1024 * 1024
 
@@ -199,6 +201,15 @@
     return [jnp.where(mask, v[None], zero).reshape(128, slots) for v in (hi, lo)]
 
 
+def hot_low_values(mask, value_row):
+    slots = value_row.shape[1]
+    value = jnp.broadcast_to(value_row, (16, slots))
+    hi = value.astype(BF16)
+    lo = ((value - hi.astype(F32)) * (1.0 / LOW)).astype(BF16)
+    zero = jnp.zeros((), BF16)
+    return [jnp.where(mask, v[None], zero).reshape(128, slots) for v in (hi, lo)]
+
+
 def hot_ones(mask):
     size = mask.shape[0] * 16
     return jnp.where(mask, jnp.ones((), BF16), jnp.zeros((), BF16)).reshape(size, mask.shape[2])
@@ -291,34 +302,37 @@
     row, lane = cell_rows(fc_ref[...], fl_ref[...])
     row_ref[...] = row
     lane_ref[...] = lane
-    for load in loads[2:7]:
+    for load in loads[2:6]:
         load.wait()
+    for f in range(4):
+        hi, lo = split(as_rows(x_ref[f]))
+        ghi[pl.ds(f * 128, 128), :] = hi
+        glo[pl.ds(f * 128, 128), :] = lo
+    counts = (5, 4, 5, 4)
+
+    def gather_four(ds):
+        for d in ds:
+
+            def store(f, q, value):
+                sbuf[d, f, pl.ds(q, 1), :] = value
+
+            gather([ghi[...], glo[...]], 4, row_ref, lane_ref, d, store)
+
+    gather_four((0, 2, 6, 8))
     for f in range(4):
         hsend[0, f] = x_ref[f, 15]
         hsend[1, f] = x_ref[f, 0]
         hsend[2, f] = x_ref[f, :, 15, :]
         hsend[3, f] = x_ref[f, :, 0, :]
+    loads[6].wait()
     hsend[0, 4] = t_ref[0, 15]
     hsend[2, 4] = t_ref[1, :, 15, :]
-    counts = (5, 4, 5, 4)
-    for f in range(4):
-        hi, lo = split(as_rows(x_ref[f]))
-        ghi[pl.ds(f * 128, 128), :] = hi
-        glo[pl.ds(f * 128, 128), :] = lo
     pl.semaphore_wait(barrier, count)
     for k in range(4):
         pl.when(neighbour(SIDES[k])[0])(halo_copy(hsend, hrecv, k, counts[k], hs, hr).start)
-
-    def gather_group(ds):
-        for d in ds:
-
-            def store(f, q, value):
-                sbuf[d, f, pl.ds(q, 1), :] = value
-
-            gather([ghi[...], glo[...]], 4, row_ref, lane_ref, d, store)
-        send_group(sbuf, rbuf, ds, fs, fr)
-
-    two_groups(gather_group)
+    send_group(sbuf, rbuf, (0, 2, 6, 8), fs, fr)
+    gather_four((1, 3, 5, 7))
+    send_group(sbuf, rbuf, (1, 3, 5, 7), fs, fr)
     for load in loads[7:]:
         load.wait()
     wait_halos(hsend, hrecv, counts, hs, hr)
@@ -397,15 +411,16 @@
             fault_rows[e, pl.ds(pl.multiple_of(d * 8, 8), 8), :] = value
 
     def scatter(d, c):
-        pair = (c, c + 1)
-        put = lanes([hot_ones(hot(lane_ref[d, pl.ds(q, 1), :], 256)) for q in pair])
-        masks = [hot(row_ref[d, pl.ds(q, 1), :], 128) for q in pair]
+        four = range(c, c + 4)
+        put = lanes([hot_ones(hot(lane_ref[d, pl.ds(q, 1), :], 256)) for q in four])
+        masks = [hot(row_ref[d, pl.ds(q, 1), :], 128) for q in four]
         his, los = [], []
         for v in range(8):
-            both = [hot_values(m, chan[v, d, pl.ds(q, 1), :]) for m, q in zip(masks, pair)]
+            both = [hot_low_values(m, chan[v, d, pl.ds(q, 1), :]) for m, q in zip(masks, four)]
             his.append(lanes([x[0] for x in both]))
             los.append(lanes([x[1] for x in both]))
-        acc[...] += dot_slots(lanes([rows(his), rows(los)]), lanes([put, put]))
+        low_put = (put * jnp.asarray(LOW, BF16)).astype(F8)
+        acc[...] += dot_slots(rows(his), put) + dot_slots(rows(los).astype(F8), low_put)
 
     def main_group(g, carry):
         wait_group(sbuf, rbuf, group(g), fs, fr)
@@ -416,8 +431,7 @@
             below = [carry_ref[v] for v in range(8)]
             for u in range(2):
                 for m in range(2):
-                    for c in (4 * m, 4 * m + 2):
-                        scatter(direction(g, h, u), c)
+                    scatter(direction(g, h, u), 4 * m)
                     below = plane(g * 8 + h * 4 + u * 2 + m, below)
             for v in range(8):
                 carry_ref[v] = below[v]

time: 31.9 us -> 30.5 us (0.956); the launches traced: 31.3 us -> 30.3 us
  Pallas kernels: 30.7 us -> 29.7 us
    pallas_call x1, Pallas kernels: 28.4 us -> 27.4 us  [per_device(): pl.pallas_call(system_kernel, out_shape=[face, f32(3, *cells), diag, faul...]
where the time goes in v3:
time: 30.5 us; the launch traced here: 30.3 us
  Pallas kernels  29.7 us (97%)
  between operations  0.64 us (2%)
    pallas_call x1, Pallas kernels, per_device(): pl.pallas_call(system_kernel, out_shape=[face, f32(3, *cells), diag, faul...  27.4 us
    pallas_call x1, Pallas kernels, per_device(): pl.pallas_call(write_kernel, out_shape=[face, f32(3, *cells), diag, fault...  2.26 us

profile of v3, /device:TPU:27, one launch (start us, length us, event | category | flops | bytes accessed | tf_op | source)
XLA Modules:
  0.0 30.3 jit_solution(4226713061971633821)
XLA Ops:
  0.6 27.4 %system.1 = (bf16[3,2,9,16,16,128]{5,4,3,2,1,0:T(8,128)(2,1)S(1)}, f32[3,16,16,128]{3,2,1,0:T(8,128)S(1)}, bf16[9,16,16,128]{3,2,1,0:T(8,128)(2,1)S(1)}, bf16[9,...) custom-call(f32[16,16,128]{2,1,0:T(8,128)} %p_hbm.1, ...), custom_call_target="tpu_custom_call" | custom-call | tf_op jit(solution)/shard_map/system/pallas_call | solution.py:619
  28.0 2.3 %write.1 = (bf16[3,2,9,16,16,128]{5,4,3,2,1,0:T(8,128)(2,1)}, f32[3,16,16,128]{3,2,1,0:T(8,128)}, bf16[9,16,16,128]{3,2,1,0:T(8,128)(2,1)}, bf16[9,1,3,3,1024]{4,3,2,1,0:T(4,128)(2,1)}, f32[16,16,128]{2,1,0:T(8,128)}) custom-call(bf16[3,2,9,16,16,128]{5,4,3,2,1,0:T(8,128)(2,1)S(1)} %get-tuple-element.21.blocks, ...), custom_call_target="tpu_custom_call" | custom-call | tf_op jit(solution)/shard_map/write/pallas_call | solution.py:681

commit v4 on v3

--- a/solution.py
+++ b/solution.py
@@ -310,7 +310,7 @@
         glo[pl.ds(f * 128, 128), :] = lo
     counts = (5, 4, 5, 4)
 
-    def gather_four(ds):
+    def gather_some(ds):
         for d in ds:
 
             def store(f, q, value):
@@ -318,7 +318,7 @@
 
             gather([ghi[...], glo[...]], 4, row_ref, lane_ref, d, store)
 
-    gather_four((0, 2, 6, 8))
+    gather_some((0, 2))
     for f in range(4):
         hsend[0, f] = x_ref[f, 15]
         hsend[1, f] = x_ref[f, 0]
@@ -328,27 +328,17 @@
     hsend[0, 4] = t_ref[0, 15]
     hsend[2, 4] = t_ref[1, :, 15, :]
     pl.semaphore_wait(barrier, count)
-    for k in range(4):
+    for k in (2, 3, 0, 1):
         pl.when(neighbour(SIDES[k])[0])(halo_copy(hsend, hrecv, k, counts[k], hs, hr).start)
-    send_group(sbuf, rbuf, (0, 2, 6, 8), fs, fr)
-    gather_four((1, 3, 5, 7))
-    send_group(sbuf, rbuf, (1, 3, 5, 7), fs, fr)
+    send_group(sbuf, rbuf, (0, 2), fs, fr)
+    gather_some((6, 8))
+    send_group(sbuf, rbuf, (6, 8), fs, fr)
+    gather_some((1, 3))
+    send_group(sbuf, rbuf, (1, 3), fs, fr)
+    gather_some((5, 7))
+    send_group(sbuf, rbuf, (5, 7), fs, fr)
     for load in loads[7:]:
         load.wait()
-    wait_halos(hsend, hrecv, counts, hs, hr)
-
-    def low_face(k, fields):
-        a = [hrecv[k, f] for f in range(4)]
-        values, _ = face_terms(
-            hrecv[k, 4], cell_terms(*a[:3]), cell_terms(*fields[:3]), a[0], fields[0], a[3], fields[3]
-        )
-        condlow_ref[k // 2] = values[2] + values[3] + values[4]
-        return lower_side(values)
-
-    for v, value in enumerate(low_face(2, [x_ref[f, :, 0, :] for f in range(4)])):
-        lowj[v] = value
-    for v, value in enumerate(low_face(0, [x_ref[f, 0] for f in range(4)])):
-        carry_ref[v] = value
     row_id = lax.broadcasted_iota(jnp.int32, (16, 128), 0)
     lane_id = lax.broadcasted_iota(jnp.int32, (16, 128), 1)
     keep_i = jnp.where(neighbour(SIDES[0])[0], 1.0, 0.0)
@@ -410,37 +400,65 @@
         for e, value in enumerate(block_rows(b, ww, wo, wg, -mw, -mo, -mgd)):
             fault_rows[e, pl.ds(pl.multiple_of(d * 8, 8), 8), :] = value
 
-    def scatter(d, c):
+    def scatter(d, c, low, high):
         four = range(c, c + 4)
         put = lanes([hot_ones(hot(lane_ref[d, pl.ds(q, 1), :], 256)) for q in four])
         masks = [hot(row_ref[d, pl.ds(q, 1), :], 128) for q in four]
         his, los = [], []
-        for v in range(8):
+        for v in range(low, high):
             both = [hot_low_values(m, chan[v, d, pl.ds(q, 1), :]) for m, q in zip(masks, four)]
             his.append(lanes([x[0] for x in both]))
             los.append(lanes([x[1] for x in both]))
         low_put = (put * jnp.asarray(LOW, BF16)).astype(F8)
-        acc[...] += dot_slots(rows(his), put) + dot_slots(rows(los).astype(F8), low_put)
-
-    def main_group(g, carry):
-        wait_group(sbuf, rbuf, group(g), fs, fr)
-        for d in group(g):
+        out = dot_slots(rows(his), put) + dot_slots(rows(los).astype(F8), low_put)
+        acc[low * 128 : high * 128, :] += out
+
+    def arrived(g, h):
+        pair = [direction(g, h, u) for u in range(2)]
+        wait_group(sbuf, rbuf, pair, fs, fr)
+        for d in pair:
             fault_terms(d)
 
-        def half(h, carry):
-            below = [carry_ref[v] for v in range(8)]
-            for u in range(2):
-                for m in range(2):
-                    scatter(direction(g, h, u), 4 * m)
-                    below = plane(g * 8 + h * 4 + u * 2 + m, below)
-            for v in range(8):
-                carry_ref[v] = below[v]
-            return carry
-
-        lax.fori_loop(0, 2, half, 0)
+    def corner_half(h, carry):
+        arrived(0, h)
+        for u in range(2):
+            for m in range(2):
+                scatter(direction(0, h, u), 4 * m, 2, 8)
         return carry
 
-    lax.fori_loop(0, 2, main_group, 0)
+    def side_half(h, carry):
+        arrived(1, h)
+        below = [carry_ref[v] for v in range(8)]
+        for u in range(2):
+            for m in range(2):
+                scatter(direction(1, h, u), 4 * m, 2, 8)
+                for n in range(2):
+                    below = plane(h * 8 + u * 4 + m * 2 + n, below)
+        for v in range(8):
+            carry_ref[v] = below[v]
+        return carry
+
+    def scatter_drives(ds):
+        for d in ds:
+            for m in range(2):
+                scatter(d, 4 * m, 0, 2)
+
+    lax.fori_loop(0, 2, corner_half, 0)
+    wait_halos(hsend, hrecv, counts, hs, hr)
+
+    def low_face(k, fields):
+        a = [hrecv[k, f] for f in range(4)]
+        values, _ = face_terms(
+            hrecv[k, 4], cell_terms(*a[:3]), cell_terms(*fields[:3]), a[0], fields[0], a[3], fields[3]
+        )
+        condlow_ref[k // 2] = values[2] + values[3] + values[4]
+        return lower_side(values)
+
+    for v, value in enumerate(low_face(2, [x_ref[f, :, 0, :] for f in range(4)])):
+        lowj[v] = value
+    for v, value in enumerate(low_face(0, [x_ref[f, 0] for f in range(4)])):
+        carry_ref[v] = value
+    lax.fori_loop(0, 2, side_half, 0)
 
     cell = pc_ref[...]
     row, lane = cell_rows(cell >> 7, cell & 127)
@@ -450,8 +468,8 @@
     put = hot_ones(hot(lane, 256))
     wacc[...] = dot_slots(lanes([rows([hi_w, hi_q]), rows([lo_w, lo_q])]), lanes([put, put]))
 
-    def sums(i):
-        return [fa[v, i] + rows_of(acc, v * 128 + i * 8) for v in range(8)]
+    def sums(i, first, last):
+        return [fa[v, i] + rows_of(acc, v * 128 + i * 8) for v in range(first, last)]
 
     def accumulation(i):
         p, sw, sg = x_ref[0, i], x_ref[1, i], x_ref[2, i]
@@ -470,7 +488,7 @@
         return cell_terms(p, sw, sg), well, drive, rock, (rock * sw * bw, rock * ob, rock * gas), (a0, a3, a6), (bw, bo, bg, rs)
 
     def residuals(i):
-        _, _, mw, mo, mgd, rw, ro, rg = sums(i)
+        mw, mo, mgd, rw, ro, rg = sums(i, 2, 8)
         c, well, drive, rock, held, slope, _ = accumulation(i)
         r0 = held[0] - 2.0 * om_ref[0, i] + rw - drive * c["mw"]
         r1 = held[1] - 2.0 * om_ref[1, i] + ro - drive * c["mo"]
@@ -484,7 +502,7 @@
         first_ref[i] = rhs / pd
 
     def diagonals(i):
-        hp, hz, mw, mo, mgd, _, _, _ = sums(i)
+        hp, hz, mw, mo, mgd = sums(i, 0, 5)
         c, well, drive, rock, held, slope, (bw, bo, bg, rs) = accumulation(i)
         dw = hp - 0.1 * hz - drive
         do = hp - 0.08 * hz - drive
@@ -510,7 +528,7 @@
     hsend2[1, 0] = first_ref[0]
     hsend2[2, 0] = first_ref[:, 15, :]
     hsend2[3, 0] = first_ref[:, 0, :]
-    for k in range(4):
+    for k in (2, 3, 0, 1):
         pl.when(neighbour(SIDES[k])[0])(halo_copy(hsend2, hrecv2, k, 1, hs2, hr2).start)
     hi, lo = split(as_rows(first_ref[...]))
     ghl[0:128, :] = hi
@@ -526,6 +544,7 @@
         send_group(sbuf2, rbuf2, ds, fs2, fr2)
 
     two_groups(gather_first)
+    two_groups(scatter_drives)
 
     def fault_out(e, carry):
         for di in range(3):
@@ -536,6 +555,9 @@
 
     lax.fori_loop(0, 9, fault_out, 0)
     plane_loop(diagonals)
+    acc2[...] = jnp.zeros_like(acc2)
+    wait_group(sbuf2, rbuf2, group(0), fs2, fr2)
+    scatter_first(group(0), row_ref, lane_ref, fcond_ref, rbuf2, acc2)
     wait_halos(hsend2, hrecv2, (1, 1, 1, 1), hs2, hr2)
 
     def faces(i):
@@ -553,13 +575,10 @@
         ck = cond_ref[2, i]
         total += ck * pltpu.roll(own, 127, 1) + pltpu.roll(ck * own, 1, 1)
         at = pl.multiple_of(i * 8, 8)
-        acc2[pl.ds(at, 8), 0:128] = total[0:8]
-        acc2[pl.ds(at, 8), 128:256] = total[8:16]
+        acc2[pl.ds(at, 8), 0:128] += total[0:8]
+        acc2[pl.ds(at, 8), 128:256] += total[8:16]
 
     plane_loop(faces)
-    acc2[128:256, :] = jnp.zeros((128, 256), F32)
-    wait_group(sbuf2, rbuf2, group(0), fs2, fr2)
-    scatter_first(group(0), row_ref, lane_ref, fcond_ref, rbuf2, acc2)
     wait_group(sbuf2, rbuf2, group(1), fs2, fr2)
     far2[...] = rbuf2[...]
 

time: 30.5 us -> 28.8 us (0.944)
  Pallas kernels: 29.7 us -> 27.7 us
    pallas_call x1, Pallas kernels: 27.4 us -> 25.4 us  [per_device(): pl.pallas_call(system_kernel, out_shape=[face, f32(3, *cells), diag, faul...]
where the time goes in v4:
time: 28.8 us; the launch traced here: 28.3 us
  Pallas kernels  27.7 us (96%)
  between operations  0.64 us (2%)
    pallas_call x1, Pallas kernels, per_device(): pl.pallas_call(system_kernel, out_shape=[face, f32(3, *cells), diag, faul...  25.4 us
    pallas_call x1, Pallas kernels, per_device(): pl.pallas_call(write_kernel, out_shape=[face, f32(3, *cells), diag, fault...  2.26 us

profile of v4, /device:TPU:27, one launch (start us, length us, event | category | flops | bytes accessed | tf_op | source)
XLA Modules:
  0.0 28.3 jit_solution(6745490297961984510)
XLA Ops:
  0.6 25.4 %system.1 = (bf16[3,2,9,16,16,128]{5,4,3,2,1,0:T(8,128)(2,1)S(1)}, f32[3,16,16,128]{3,2,1,0:T(8,128)S(1)}, bf16[9,16,16,128]{3,2,1,0:T(8,128)(2,1)S(1)}, bf16[9,...) custom-call(f32[16,16,128]{2,1,0:T(8,128)} %p_hbm.1, ...), custom_call_target="tpu_custom_call" | custom-call | tf_op jit(solution)/shard_map/system/pallas_call | solution.py:638
  26.1 2.3 %write.1 = (bf16[3,2,9,16,16,128]{5,4,3,2,1,0:T(8,128)(2,1)}, f32[3,16,16,128]{3,2,1,0:T(8,128)}, bf16[9,16,16,128]{3,2,1,0:T(8,128)(2,1)}, bf16[9,1,3,3,1024]{4,3,2,1,0:T(4,128)(2,1)}, f32[16,16,128]{2,1,0:T(8,128)}) custom-call(bf16[3,2,9,16,16,128]{5,4,3,2,1,0:T(8,128)(2,1)S(1)} %get-tuple-element.21.blocks, ...), custom_call_target="tpu_custom_call" | custom-call | tf_op jit(solution)/shard_map/write/pallas_call | solution.py:700

commit v5 on v4

--- a/solution.py
+++ b/solution.py
@@ -254,11 +254,11 @@
 
 def plane_loop(body):
     def step(i, carry):
-        body(2 * i)
-        body(2 * i + 1)
+        for n in range(4):
+            body(4 * i + n)
         return carry
 
-    lax.fori_loop(0, 8, step, 0)
+    lax.fori_loop(0, 4, step, 0)
 
 
 def rows_of(ref, start):

time: 28.8 us -> 28.5 us (0.990)
  Pallas kernels: 27.7 us -> 27.3 us
    pallas_call x1, Pallas kernels: 25.4 us -> 25 us  [per_device(): pl.pallas_call(system_kernel, out_shape=[face, f32(3, *cells), diag, faul...]
where the time goes in v5:
time: 28.5 us; the launch traced here: 27.9 us
  Pallas kernels  27.3 us (96%)
  between operations  0.64 us (2%)
    pallas_call x1, Pallas kernels, per_device(): pl.pallas_call(system_kernel, out_shape=[face, f32(3, *cells), diag, faul...  25 us
    pallas_call x1, Pallas kernels, per_device(): pl.pallas_call(write_kernel, out_shape=[face, f32(3, *cells), diag, fault...  2.26 us

profile of v5, /device:TPU:27, one launch (start us, length us, event | category | flops | bytes accessed | tf_op | source)
XLA Modules:
  0.0 27.9 jit_solution(14175859733645651183)
XLA Ops:
  0.6 25.0 %system.1 = (bf16[3,2,9,16,16,128]{5,4,3,2,1,0:T(8,128)(2,1)S(1)}, f32[3,16,16,128]{3,2,1,0:T(8,128)S(1)}, bf16[9,16,16,128]{3,2,1,0:T(8,128)(2,1)S(1)}, bf16[9,...) custom-call(f32[16,16,128]{2,1,0:T(8,128)} %p_hbm.1, ...), custom_call_target="tpu_custom_call" | custom-call | tf_op jit(solution)/shard_map/system/pallas_call | solution.py:638
  25.7 2.3 %write.1 = (bf16[3,2,9,16,16,128]{5,4,3,2,1,0:T(8,128)(2,1)}, f32[3,16,16,128]{3,2,1,0:T(8,128)}, bf16[9,16,16,128]{3,2,1,0:T(8,128)(2,1)}, bf16[9,1,3,3,1024]{4,3,2,1,0:T(4,128)(2,1)}, f32[16,16,128]{2,1,0:T(8,128)}) custom-call(bf16[3,2,9,16,16,128]{5,4,3,2,1,0:T(8,128)(2,1)S(1)} %get-tuple-element.21.blocks, ...), custom_call_target="tpu_custom_call" | custom-call | tf_op jit(solution)/shard_map/write/pallas_call | solution.py:700
